TPU v7x, 32 devices: a whole 2x2x4 slice. The times are simulated.
32 devices in a mesh: parts: 2 (over x), blk: 8 (over z, y), pair: 2 (over core).
Axes of the slice: x: 2, y: 2, z: 4, core: 2. Of those that a mesh axis runs over, the one named last changes fastest.
Arguments:
- queries: bfloat16 [28672, 768], P(('parts', 'blk', 'pair')), parts along dimension 0, may hold values from -50 to 50, as said below
- key_rows: bfloat16 [2048, 768], P(('parts', 'blk', 'pair')), parts along dimension 0, may hold values from -12 to 12, as said below
- label_rows: bfloat16 [2048, 1000], P(('parts', 'blk', 'pair')), parts along dimension 0, may hold values from -16 to 16
Outputs:
- corrected: bfloat16 [28672, 1000], P(('parts', 'blk', 'pair')), parts along dimension 0
There are 2 independent parts, one for each index of `parts`. A program takes and returns all parts, laid end to end along the dimension named above; each array names one. Nothing has to cross between parts.
Inputs may be any that keep to these rules, and one draw needn't show every extreme that they name: `queries`: query embeddings; rows have different scales. `key_rows`: corpus embeddings; rows have different scales.
All inputs are finite; a program needn't handle non-finite values.
Results may differ from a plain program's by a relative error of at most 0.0045.
Values may be sent and summed in bfloat16 or wider, within the bound.
No kernel may reach another device: no remote copies, remote signals or barrier semaphores. Data moves between devices by JAX's collectives and lax.ppermute only.
A program may use at most 128 MiB of HBM per device.

v0:
```python
import jax
import jax.numpy as jnp
from jax import lax
from jax.sharding import PartitionSpec as P

E = 768


def absorb_block(query_rows, carry, fragment):
    run_max, totals, weighted = carry
    key_part, label_part = fragment
    scores = lax.dot_general(
        query_rows, key_part, (((1,), (1,)), ((), ())), preferred_element_type=jnp.float32
    ) * E ** (-0.5)
    new_max = jnp.maximum(run_max, jnp.max(scores, axis=1))
    factor = jnp.exp(run_max - new_max)
    weights = jnp.exp(scores - new_max[:, None])
    totals = totals * factor + jnp.sum(weights, axis=1)
    weighted = weighted * factor[:, None] + jnp.dot(
        weights.astype(jnp.bfloat16), label_part, preferred_element_type=jnp.float32
    )
    return (new_max, totals, weighted)


def absorb(query_rows, carry, fragment):
    key_part, label_part = fragment
    count = key_part.shape[0]
    if count > 1024 and count % 1024 == 0:

        def update(state, pieces):
            return (absorb_block(query_rows, state, pieces), None)

        stacked = (
            key_part.reshape(count // 1024, 1024, key_part.shape[1]),
            label_part.reshape(count // 1024, 1024, label_part.shape[1]),
        )
        result, unused = lax.scan(update, carry, stacked)
        return result
    return absorb_block(query_rows, carry, (key_part, label_part))


def start_state(query_rows, classes):
    count = query_rows.shape[0]
    return (
        jnp.full((count,), -jnp.inf, jnp.float32),
        jnp.zeros((count,), jnp.float32),
        jnp.zeros((count, classes), jnp.float32),
    )


def on_device(queries, key_rows, label_rows):
    classes = label_rows.shape[1]
    chip_keys, chip_labels = (
        lax.all_gather(key_rows, "pair", axis=0, tiled=True),
        lax.all_gather(label_rows, "pair", axis=0, tiled=True),
    )
    run_max, totals, weighted = absorb(
        queries,
        start_state(queries, classes),
        (
            lax.all_gather(chip_keys, "blk", axis=0, tiled=True),
            lax.all_gather(chip_labels, "blk", axis=0, tiled=True),
        ),
    )
    return (weighted / totals[:, None]).astype(jnp.bfloat16)


def solution(mesh):
    in_specs = (
        P(("parts", "blk", "pair"), None),
        P(("parts", "blk", "pair"), None),
        P(("parts", "blk", "pair"), None),
    )
    out_specs = P(("parts", "blk", "pair"), None)
    return jax.shard_map(
        on_device, mesh=mesh, in_specs=in_specs, out_specs=out_specs, check_vma=False
    )
```

profile of v0, /device:TPU:0, one launch (start us, length us, event | category | flops | bytes accessed | tf_op | source)
XLA Modules:
  0.0 120.7 jit_solution(16346918333426672644)
XLA Ops:
  6.5 0.0 copy-start
  6.5 0.0 all-gather.3.cloned.1.call-start
  6.5 3.9 %all_gather.12 = bf16[128,768]{1,0:T(8,128)(2,1)} all-gather(bf16[64,768]{1,0:T(8,128)(2,1)} %param.4), channel_id=1, replica_groups=mesh['parts'=2,'blk'=8,'pair'=2] {'pair'}, dimensions={0}, use_global_device_ids=true | all-gather | bytes 294912 | tf_op jit(solution)/shard_map/all_gather | solution.py:54
  10.4 0.0 all-gather.3.cloned.1.call-update
  10.5 0.0 all-gather.5.cloned.1.call-start
  10.5 3.6 %all_gather.14 = bf16[128,1000]{1,0:T(8,128)(2,1)} all-gather(bf16[64,1000]{1,0:T(8,128)(2,1)} %param.5), channel_id=1, replica_groups=mesh['parts'=2,'blk'=8,'pair'=2] {'pair'}, dimensions={0}, use_global_device_ids=true | all-gather | bytes 384000 | tf_op jit(solution)/shard_map/all_gather | solution.py:55
  14.1 0.0 all-gather.5.cloned.1.call-update
  14.1 43.1 %all-gather.3.cloned.1.call-done = bf16[1024,768]{1,0:T(8,128)(2,1)} async-done(((bf16[128,768]{1,0:T(8,128)(2,1)}), bf16[1024,768]{1,0:T(8,128)(2,1)}) %all-gather.3.cloned.1.call-update) | async-done | bytes 1572880 | tf_op jit(solution)/shard_map/all_gather | solution.py:61
  57.2 0.0 copy-done
  57.2 3.1 %multiply_reduce_fusion = (f32[896]{0:T(1024)S(1)}, f32[896,1024]{1,0:T(8,128)S(1)}) fusion(bf16[896,768]{1,0:T(8,128)(2,1)S(1)} %copy-done, bf16[1024,768]{1,0:T(8,128)(2,1)} %all-gather.3.cloned.1.call-done), kind=kOutput, calls=%fused_computation.2 | convolution fusion | flops 1411120256 | bytes 6622720 | tf_op jit(solution)/shard_map/dot_general | solution.py:12
  60.3 0.0 copy-start.1
  60.3 1.8 %copy-done.1 = f32[896,1024]{1,0:T(8,128)} copy-done((f32[896,1024]{1,0:T(8,128)}, f32[896,1024]{1,0:T(8,128)S(1)}, u32[]{:S(2)}) %copy-start.1) | copy-done | bytes 3670040
  62.1 0.9 fusion
  63.0 44.5 %all-gather.5.cloned.1.call-done = bf16[1024,1000]{1,0:T(8,128)(2,1)} async-done(((bf16[128,1000]{1,0:T(8,128)(2,1)}), bf16[1024,1000]{1,0:T(8,128)(2,1)}) %all-gather.5.cloned.1.call-update) | async-done | bytes 2048016 | tf_op jit(solution)/shard_map/all_gather | solution.py:62
  107.5 6.4 %divide_convert_fusion = bf16[896,1000]{0,1:T(8,128)(2,1)} fusion(f32[896]{0:T(1024)S(1)} %get-tuple-element.6, f32[896]{0:T(1024)S(1)} %get-tuple-element.5, bf16[1024,1000]{1,0:T(8,128)(2,1)} %all-gather.5.cloned.1.call-done, f32[896,1024]{1,0:T(8,128)} %copy-done.1, f32[896]{0:T(1024)S(1)} %get-tuple-element.7), kind=kOutput, calls=%fused_computation.1 | convolution fusion | flops 1840448512 | bytes 7520768 | tf_op jit(solution)/shard_map/dot_general | solution.py:19
  (1 shorter events, 0.0 us)
Async XLA Ops:
  6.5 50.7 %copy-start = (bf16[896,768]{1,0:T(8,128)(2,1)S(1)}, bf16[896,768]{1,0:T(8,128)(2,1)}, u32[]{:S(2)}) copy-start(bf16[896,768]{1,0:T(8,128)(2,1)} %param.3) | copy-start | bytes 4128772
  6.5 50.7 %all-gather.3.cloned.1.call-start = ((), (), s32[]{:S(2)}) async-start(), calls=%async_computation | async-start | bytes 1769472 | tf_op jit(solution)/shard_map/all_gather | solution.py:61
  10.5 97.0 %all-gather.5.cloned.1.call-start = ((), (), s32[]{:S(2)}) async-start(), calls=%async_computation.1 | async-start | bytes 2359296 | tf_op jit(solution)/shard_map/all_gather | solution.py:62
  60.3 1.8 %copy-start.1 = (f32[896,1024]{1,0:T(8,128)}, f32[896,1024]{1,0:T(8,128)S(1)}, u32[]{:S(2)}) copy-start(f32[896,1024]{1,0:T(8,128)S(1)} %get-tuple-element.8) | copy-start | bytes 11010052
Sparse Core Ops, SparseCore 0:
  10.6 46.5 all-gather.2
  59.3 48.0 all-gather.4
where the time goes:
time: 121 us
  waiting for transfers between devices  87.6 us (72%)
  between operations  13.4 us (11%)
  matrix products  9.51 us (8%)
  blocking collectives  7.46 us (6%)
  local copies, waits for them, and re-layouts  1.79 us (1%)
    all_gather x1, waiting for transfers between devices, on_device(): lax.all_gather(chip_labels, 'blk', axis=0, tiled=True)  44.5 us
    all_gather x1, waiting for transfers between devices, on_device(): lax.all_gather(chip_keys, 'blk', axis=0, tiled=True)  43.1 us
    dot_general x1, matrix products, absorb_block(): jnp.dot(weights.astype(jnp.bfloat16), label_part, preferred_element_type=...  6.41 us
    all_gather x1, blocking collectives, on_device(): lax.all_gather(key_rows, 'pair', axis=0, tiled=True)  3.9 us
    all_gather x1, blocking collectives, on_device(): lax.all_gather(label_rows, 'pair', axis=0, tiled=True)  3.56 us
    dot_general x1, matrix products, absorb_block(): lax.dot_general(query_rows, key_part, (((1,), (1,)), ((), ())), preferred...  3.11 us
  transfers between devices with their start and end apart: 2, of which 2 were waited for; matrix products, arithmetic and copies ran while one was open for 3% of the time, Pallas kernels for 0%

commit v1 on v0

v1 whole, which is shorter than its diff:
```python
import jax
import jax.numpy as jnp
from jax import lax
from jax.experimental import pallas as pl
from jax.experimental.pallas import tpu as pltpu
from jax.sharding import PartitionSpec as P

AXES = ("blk", "pair")


def ring_of(chips):
    if chips == 8:
        return [0, 2, 4, 6, 7, 5, 3, 1]
    return list(range(chips))


def hop(ring, shift, swap):
    n, out = len(ring), []
    for place, chip in enumerate(ring):
        for core in range(2):
            step = shift if core == 0 else -shift
            out.append((chip * 2 + core, ring[(place + step) % n] * 2 + (core ^ swap)))
    return out


def attend(width, scale, count, *refs):
    q_ref, pieces, out_ref = refs[0], refs[1 : 1 + count], refs[1 + count]
    keys = jnp.concatenate([p[:, :width] for p in pieces], axis=0)
    labels = jnp.concatenate([p[:, width:] for p in pieces], axis=0)
    rows = q_ref.shape[0]
    for low in range(0, rows, 128):
        high = min(low + 128, rows)
        scores = (
            lax.dot_general(
                keys, q_ref[low:high, :], (((1,), (1,)), ((), ())), preferred_element_type=jnp.float32
            )
            * scale
        )
        weights = jnp.exp(scores - jnp.max(scores, axis=0, keepdims=True))
        totals = jnp.sum(weights, axis=0, keepdims=True)
        weighted = lax.dot_general(
            labels, weights.astype(jnp.bfloat16), (((0,), (0,)), ((), ())), preferred_element_type=jnp.float32
        )
        out_ref[:, low:high] = (weighted / totals).astype(jnp.bfloat16)


def on_device(queries, key_rows, label_rows, chips):
    width, classes = key_rows.shape[1], label_rows.shape[1]
    half = key_rows.shape[0]
    ring = ring_of(chips)
    same, cross, swap = hop(ring, 1, 0), hop(ring, -1, 1), hop(ring, 0, 1)

    def send(x, pairs):
        return lax.ppermute(x, AXES, pairs)

    def beside(k, l):
        return jnp.concatenate([k, l], axis=1)

    pieces = [beside(key_rows, label_rows), beside(send(key_rows, swap), send(label_rows, swap))]
    first = beside(send(key_rows, same), send(label_rows, same))
    second = beside(send(key_rows, cross), send(label_rows, cross))
    for step in range(1, chips // 2 + 1):
        last = step == chips // 2
        here = [first] if last else [first, second]
        pieces += here + [send(x, swap) for x in here]
        if not last:
            first = send(first, same)
            if step + 1 < chips // 2:
                second = send(second, same)
    rows = queries.shape[0]
    out = pl.pallas_call(
        lambda *refs: attend(width, width**-0.5, len(pieces), *refs),
        out_shape=jax.ShapeDtypeStruct((classes, rows), jnp.bfloat16),
        in_specs=[pl.BlockSpec(memory_space=pltpu.VMEM)] * (1 + len(pieces)),
        out_specs=pl.BlockSpec(memory_space=pltpu.VMEM),
        compiler_params=pltpu.CompilerParams(vmem_limit_bytes=56 * 2**20),
    )(queries, *pieces)
    return out.T


def solution(mesh):
    chips = mesh.shape["blk"]
    spec = P(("parts", "blk", "pair"), None)
    return jax.shard_map(
        lambda q, k, l: on_device(q, k, l, chips),
        mesh=mesh,
        in_specs=(spec, spec, spec),
        out_specs=spec,
        check_vma=False,
    )
```

time: 121 us -> 40.8 us (0.34)
  waiting for transfers between devices: 87.6 us -> 10.2 us
  starting transfers between devices: 0.04 us -> 15.8 us
  between operations: 13.4 us -> 0.18 us
  Pallas kernels: 0 us -> 11 us
  matrix products: 9.51 us -> 0 us
  blocking collectives: 7.46 us -> 0 us
  other arithmetic: 0.86 us -> 2.42 us
    all_gather x2 -> x0, waiting for transfers between devices: 87.6 us -> none  [the longest x1 44.5 us: on_device(): lax.all_gather(chip_labels, 'blk', axis=0, tiled=True)]
    ppermute x0 -> x18, starting transfers between devices: none -> 15.8 us  [send(): return lax.ppermute(x, AXES, pairs)]
    pallas_call x0 -> x1, Pallas kernels: none -> 11 us  [on_device(): pl.pallas_call(lambda *refs: attend(width, width ** (-0.5), len(pieces),...]
    ppermute x0 -> x18, waiting for transfers between devices: none -> 10.2 us  [send(): return lax.ppermute(x, AXES, pairs)]
    dot_general x2 -> x0, matrix products: 9.51 us -> none  [the longest x1 6.41 us: absorb_block(): jnp.dot(weights.astype(jnp.bfloat16), label_part, preferred_element_type=...]
    all_gather x2 -> x0, blocking collectives: 7.46 us -> none  [the longest x1 3.9 us: on_device(): lax.all_gather(key_rows, 'pair', axis=0, tiled=True)]
    concatenate x0 -> x2, other arithmetic: none -> 2.42 us  [beside(): return jnp.concatenate([k, l], axis=1)]
  transfers between devices with their start and end apart: 2 -> 18, of which waited for: 2 -> 7; matrix products, arithmetic and copies ran while one was open for 3% -> 6% of each run, Pallas kernels for 0% -> 0%
where the time goes in v1:
time: 40.8 us; the launch traced here: 40.5 us
  starting transfers between devices  15.8 us (39%)
  Pallas kernels  11 us (27%)
  waiting for transfers between devices  10.2 us (25%)
  other arithmetic  2.42 us (6%)
  local copies, waits for them, and re-layouts  0.87 us (2%)
    ppermute x18, starting transfers between devices, send(): return lax.ppermute(x, AXES, pairs)  15.8 us
    pallas_call x1, Pallas kernels, on_device(): pl.pallas_call(lambda *refs: attend(width, width ** (-0.5), len(pieces),...  11 us
    ppermute x18, waiting for transfers between devices, send(): return lax.ppermute(x, AXES, pairs)  10.2 us
    concatenate x2, other arithmetic, beside(): return jnp.concatenate([k, l], axis=1)  2.42 us
    unnamed x30, local copies, waits for them, and re-layouts  0.85 us
  transfers between devices with their start and end apart: 18, of which 7 were waited for; matrix products, arithmetic and copies ran while one was open for 6% of the time, Pallas kernels for 0%

profile of v1, /device:TPU:0, one launch (start us, length us, event | category | flops | bytes accessed | tf_op | source)
XLA Modules:
  0.0 40.5 jit_solution(15040507760949605629)
XLA Ops:
  0.0 3.0 %collective-permute-start.2 = (bf16[64,768]{1,0:T(8,128)(2,1)}, bf16[64,768]{1,0:T(8,128)(2,1)S(1)}, u32[]{:S(2)}, u32[]{:S(2)}) collective-permute-start(bf16[64,768]{1,0:T(8,128)(2,1)} %param.4), channel_id=1, source_target_pairs={{0,4},{1,3},{4,8},{5,1},{8,12},{9,5},{12,14},{13,9},{14,10},{15,13... | collective-permute-start | bytes 294920 | tf_op jit(solution)/shard_map/ppermute | solution.py:54
  3.0 1.6 %collective-permute-start.3 = (bf16[64,1000]{1,0:T(8,128)(2,1)}, bf16[64,1000]{1,0:T(8,128)(2,1)S(1)}, u32[]{:S(2)}, u32[]{:S(2)}) collective-permute-start(bf16[64,1000]{1,0:T(8,128)(2,1)} %param.5), channel_id=1, source_target_pairs={{0,4},{1,3},{4,8},{5,1},{8,12},{9,5},{12,14},{13,9},{14,10},{15,13... | collective-permute-start | bytes 384008 | tf_op jit(solution)/shard_map/ppermute | solution.py:54
  4.6 0.4 collective-permute-start.4
  5.0 1.3 %collective-permute-start.5 = (bf16[64,1000]{1,0:T(8,128)(2,1)}, bf16[64,1000]{1,0:T(8,128)(2,1)S(1)}, u32[]{:S(2)}, u32[]{:S(2)}) collective-permute-start(bf16[64,1000]{1,0:T(8,128)(2,1)} %param.5), channel_id=1, source_target_pairs={{0,3},{1,4},{4,1},{5,8},{8,5},{9,12},{12,9},{13,14},{14,13},{15,10... | collective-permute-start | bytes 384008 | tf_op jit(solution)/shard_map/ppermute | solution.py:54
  6.4 2.2 %collective-permute-done.3 = bf16[64,1000]{1,0:T(8,128)(2,1)S(1)} collective-permute-done((bf16[64,1000]{1,0:T(8,128)(2,1)}, bf16[64,1000]{1,0:T(8,128)(2,1)S(1)}, u32[]{:S(2)}, u32[]{:S(2)}) %collective-permute-start.3) | collective-permute-done | bytes 128032 | tf_op jit(solution)/shard_map/ppermute | solution.py:54
  8.6 1.6 %collective-permute-start.8 = (bf16[64,1768]{1,0:T(8,128)(2,1)S(1)}, bf16[64,1768]{1,0:T(8,128)(2,1)S(1)}, u32[]{:S(2)}, u32[]{:S(2)}) collective-permute-start(bf16[64,1768]{1,0:T(8,128)(2,1)S(1)} %constant_dynamic-update-slice_fusion.refs_3_), channel_id=1, source_target_pairs={{0,4},{1,3},{4,8},{5,1},{8,12},{9,5},{12,14},{13,9},{14,10},{15,13... | collective-permute-start | bytes 678920 | tf_op jit(solution)/shard_map/ppermute | solution.py:54
  10.3 0.4 collective-permute-done.5
  10.7 1.6 %collective-permute-start.9 = (bf16[64,1768]{1,0:T(8,128)(2,1)S(1)}, bf16[64,1768]{1,0:T(8,128)(2,1)S(1)}, u32[]{:S(2)}, u32[]{:S(2)}) collective-permute-start(bf16[64,1768]{1,0:T(8,128)(2,1)S(1)} %constant_dynamic-update-slice_fusion.2.refs_4_), channel_id=1, source_target_pairs={{0,4},{1,3},{4,8},{5,1},{8,12},{9,5},{12,14},{13,9},{14,10},{15,13... | collective-permute-start | bytes 678920 | tf_op jit(solution)/shard_map/ppermute | solution.py:54
  12.3 2.4 %collective-permute-done.8.refs_7_ = bf16[64,1768]{1,0:T(8,128)(2,1)S(1)} collective-permute-done((bf16[64,1768]{1,0:T(8,128)(2,1)S(1)}, bf16[64,1768]{1,0:T(8,128)(2,1)S(1)}, u32[]{:S(2)}, u32[]{:S(2)}) %collective-permute-start.8) | collective-permute-done | bytes 226336 | tf_op jit(solution)/shard_map/ppermute | solution.py:54
  14.7 1.6 %collective-permute-start.12 = (bf16[64,1768]{1,0:T(8,128)(2,1)S(1)}, bf16[64,1768]{1,0:T(8,128)(2,1)S(1)}, u32[]{:S(2)}, u32[]{:S(2)}) collective-permute-start(bf16[64,1768]{1,0:T(8,128)(2,1)S(1)} %collective-permute-done.8.refs_7_), channel_id=1, source_target_pairs={{0,4},{1,3},{4,8},{5,1},{8,12},{9,5},{12,14},{13,9},{14,10},{15,13... | collective-permute-start | bytes 678920 | tf_op jit(solution)/shard_map/ppermute | solution.py:54
  16.3 0.5 %collective-permute-start.1 = (bf16[64,1000]{1,0:T(8,128)(2,1)}, bf16[64,1000]{1,0:T(8,128)(2,1)S(1)}, u32[]{:S(2)}, u32[]{:S(2)}) collective-permute-start(bf16[64,1000]{1,0:T(8,128)(2,1)} %param.5), channel_id=1, source_target_pairs={{0,1},{1,0},{4,5},{5,4},{8,9},{9,8},{12,13},{13,12},{14,15},{15,14... | collective-permute-start | bytes 384008 | tf_op jit(solution)/shard_map/ppermute | solution.py:54
  16.8 1.0 %collective-permute-done = bf16[64,768]{1,0:T(8,128)(2,1)S(1)} collective-permute-done((bf16[64,768]{1,0:T(8,128)(2,1)}, bf16[64,768]{1,0:T(8,128)(2,1)S(1)}, u32[]{:S(2)}, u32[]{:S(2)}) %collective-permute-start) | collective-permute-done | bytes 98336 | tf_op jit(solution)/shard_map/ppermute | solution.py:54
  17.8 0.2 collective-permute-start.7
  18.0 1.7 %collective-permute-start.13 = (bf16[64,1768]{1,0:T(8,128)(2,1)S(1)}, bf16[64,1768]{1,0:T(8,128)(2,1)S(1)}, u32[]{:S(2)}, u32[]{:S(2)}) collective-permute-start(bf16[64,1768]{1,0:T(8,128)(2,1)S(1)} %collective-permute-done.9.refs_8_), channel_id=1, source_target_pairs={{0,4},{1,3},{4,8},{5,1},{8,12},{9,5},{12,14},{13,9},{14,10},{15,13... | collective-permute-start | bytes 678920 | tf_op jit(solution)/shard_map/ppermute | solution.py:54
  19.7 1.4 %collective-permute-done.12.refs_11_ = bf16[64,1768]{1,0:T(8,128)(2,1)S(1)} collective-permute-done((bf16[64,1768]{1,0:T(8,128)(2,1)S(1)}, bf16[64,1768]{1,0:T(8,128)(2,1)S(1)}, u32[]{:S(2)}, u32[]{:S(2)}) %collective-permute-start.12) | collective-permute-done | bytes 226336 | tf_op jit(solution)/shard_map/ppermute | solution.py:54
  21.1 1.2 %collective-permute-start.16 = (bf16[64,1768]{1,0:T(8,128)(2,1)S(1)}, bf16[64,1768]{1,0:T(8,128)(2,1)S(1)}, u32[]{:S(2)}, u32[]{:S(2)}) collective-permute-start(bf16[64,1768]{1,0:T(8,128)(2,1)S(1)} %collective-permute-done.12.refs_11_), channel_id=1, source_target_pairs={{0,4},{1,3},{4,8},{5,1},{8,12},{9,5},{12,14},{13,9},{14,10},{15,13... | collective-permute-start | bytes 678920 | tf_op jit(solution)/shard_map/ppermute | solution.py:54
  22.3 1.7 %pad_maximum_fusion.refs_1_ = bf16[64,1768]{1,0:T(8,128)(2,1)} fusion(bf16[64,1000]{1,0:T(8,128)(2,1)} %param.5, bf16[64,768]{1,0:T(8,128)(2,1)} %param.4), kind=kLoop, calls=%fused_computation | loop fusion | flops 452608 | bytes 452608 | tf_op jit(solution)/shard_map/concatenate | solution.py:57
  24.0 0.5 %collective-permute-start.11 = (bf16[64,1768]{1,0:T(8,128)(2,1)S(1)}, bf16[64,1768]{1,0:T(8,128)(2,1)S(1)}, u32[]{:S(2)}, u32[]{:S(2)}) collective-permute-start(bf16[64,1768]{1,0:T(8,128)(2,1)S(1)} %collective-permute-done.9.refs_8_), channel_id=1, source_target_pairs={{0,1},{1,0},{4,5},{5,4},{8,9},{9,8},{12,13},{13,12},{14,15},{15,14... | collective-permute-start | bytes 678920 | tf_op jit(solution)/shard_map/ppermute | solution.py:54
  24.6 0.4 %collective-permute-start.15 = (bf16[64,1768]{1,0:T(8,128)(2,1)S(1)}, bf16[64,1768]{1,0:T(8,128)(2,1)S(1)}, u32[]{:S(2)}, u32[]{:S(2)}) collective-permute-start(bf16[64,1768]{1,0:T(8,128)(2,1)S(1)} %collective-permute-done.13.refs_12_), channel_id=1, source_target_pairs={{0,1},{1,0},{4,5},{5,4},{8,9},{9,8},{12,13},{13,12},{14,15},{15,14... | collective-permute-start | bytes 678920 | tf_op jit(solution)/shard_map/ppermute | solution.py:54
  25.0 2.1 %collective-permute-done.16.refs_15_ = bf16[64,1768]{1,0:T(8,128)(2,1)S(1)} collective-permute-done((bf16[64,1768]{1,0:T(8,128)(2,1)S(1)}, bf16[64,1768]{1,0:T(8,128)(2,1)S(1)}, u32[]{:S(2)}, u32[]{:S(2)}) %collective-permute-start.16) | collective-permute-done | bytes 226336 | tf_op jit(solution)/shard_map/ppermute | solution.py:54
  27.1 0.8 %pad_maximum_fusion.1.refs_2_ = bf16[64,1768]{1,0:T(8,128)(2,1)} fusion(bf16[64,1000]{1,0:T(8,128)(2,1)S(1)} %collective-permute-done.1, bf16[64,768]{1,0:T(8,128)(2,1)S(1)} %collective-permute-done), kind=kLoop, calls=%fused_computation.1 | loop fusion | flops 452608 | bytes 452608 | tf_op jit(solution)/shard_map/concatenate | solution.py:57
  27.9 0.7 %collective-permute-done.17.refs_16_ = bf16[64,1768]{1,0:T(8,128)(2,1)S(1)} collective-permute-done((bf16[64,1768]{1,0:T(8,128)(2,1)S(1)}, bf16[64,1768]{1,0:T(8,128)(2,1)S(1)}, u32[]{:S(2)}, u32[]{:S(2)}) %collective-permute-start.17) | collective-permute-done | bytes 226336 | tf_op jit(solution)/shard_map/ppermute | solution.py:54
  28.8 0.7 %copy-done.13 = bf16[64,1768]{1,0:T(8,128)(2,1)} copy-done((bf16[64,1768]{1,0:T(8,128)(2,1)}, bf16[64,1768]{1,0:T(8,128)(2,1)S(1)}, u32[]{:S(2)}) %copy-start.13) | copy-done | bytes 226328
  29.5 11.0 %shard_map.37 = bf16[1000,896]{1,0:T(8,128)(2,1)} custom-call(bf16[896,768]{1,0:T(8,128)(2,1)} %refs_0_.1, bf16[64,1768]{1,0:T(8,128)(2,1)} %pad_maximum_fusion.refs_1_, bf16[64,1768]{1,0:T(8,128)(2,1)} %pad_maximum_fusion.1.refs_2_, bf16[64,1768]{1,0:T(8,128)(2,1)} %copy-done, bf16[64,1768]{1,0:T(8,128)(2,1)} %copy-done.1, bf16[64,1768]{1,0:T(8,128)(2,1)} %copy-done.5, ...), custom_call_target="tpu_custom_call" | custom-call | tf_op jit(solution)/shard_map/pallas_call | solution.py:71
  (47 shorter events, 0.3 us)
Async XLA Ops:
  0.0 6.4 %collective-permute-start.2 = (bf16[64,768]{1,0:T(8,128)(2,1)}, bf16[64,768]{1,0:T(8,128)(2,1)S(1)}, u32[]{:S(2)}, u32[]{:S(2)}) collective-permute-start(bf16[64,768]{1,0:T(8,128)(2,1)} %param.4), channel_id=1, source_target_pairs={{0,4},{1,3},{4,8},{5,1},{8,12},{9,5},{12,14},{13,9},{14,10},{15,13... | collective-permute-start | bytes 294920 | tf_op jit(solution)/shard_map/ppermute | solution.py:54
  3.0 5.6 %collective-permute-start.3 = (bf16[64,1000]{1,0:T(8,128)(2,1)}, bf16[64,1000]{1,0:T(8,128)(2,1)S(1)}, u32[]{:S(2)}, u32[]{:S(2)}) collective-permute-start(bf16[64,1000]{1,0:T(8,128)(2,1)} %param.5), channel_id=1, source_target_pairs={{0,4},{1,3},{4,8},{5,1},{8,12},{9,5},{12,14},{13,9},{14,10},{15,13... | collective-permute-start | bytes 384008 | tf_op jit(solution)/shard_map/ppermute | solution.py:54
  4.6 5.7 %collective-permute-start.4 = (bf16[64,768]{1,0:T(8,128)(2,1)}, bf16[64,768]{1,0:T(8,128)(2,1)S(1)}, u32[]{:S(2)}, u32[]{:S(2)}) collective-permute-start(bf16[64,768]{1,0:T(8,128)(2,1)} %param.4), channel_id=1, source_target_pairs={{0,3},{1,4},{4,1},{5,8},{8,5},{9,12},{12,9},{13,14},{14,13},{15,10... | collective-permute-start | bytes 294920 | tf_op jit(solution)/shard_map/ppermute | solution.py:54
  5.0 5.7 %collective-permute-start.5 = (bf16[64,1000]{1,0:T(8,128)(2,1)}, bf16[64,1000]{1,0:T(8,128)(2,1)S(1)}, u32[]{:S(2)}, u32[]{:S(2)}) collective-permute-start(bf16[64,1000]{1,0:T(8,128)(2,1)} %param.5), channel_id=1, source_target_pairs={{0,3},{1,4},{4,1},{5,8},{8,5},{9,12},{12,9},{13,14},{14,13},{15,10... | collective-permute-start | bytes 384008 | tf_op jit(solution)/shard_map/ppermute | solution.py:54
  8.6 20.0 %copy-start = (bf16[64,1768]{1,0:T(8,128)(2,1)}, bf16[64,1768]{1,0:T(8,128)(2,1)S(1)}, u32[]{:S(2)}) copy-start(bf16[64,1768]{1,0:T(8,128)(2,1)S(1)} %constant_dynamic-update-slice_fusion.refs_3_) | copy-start | bytes 678916
  8.6 6.1 %collective-permute-start.8 = (bf16[64,1768]{1,0:T(8,128)(2,1)S(1)}, bf16[64,1768]{1,0:T(8,128)(2,1)S(1)}, u32[]{:S(2)}, u32[]{:S(2)}) collective-permute-start(bf16[64,1768]{1,0:T(8,128)(2,1)S(1)} %constant_dynamic-update-slice_fusion.refs_3_), channel_id=1, source_target_pairs={{0,4},{1,3},{4,8},{5,1},{8,12},{9,5},{12,14},{13,9},{14,10},{15,13... | collective-permute-start | bytes 678920 | tf_op jit(solution)/shard_map/ppermute | solution.py:54
  10.7 17.9 %copy-start.1 = (bf16[64,1768]{1,0:T(8,128)(2,1)}, bf16[64,1768]{1,0:T(8,128)(2,1)S(1)}, u32[]{:S(2)}) copy-start(bf16[64,1768]{1,0:T(8,128)(2,1)S(1)} %constant_dynamic-update-slice_fusion.2.refs_4_) | copy-start | bytes 678916
  10.7 7.3 %collective-permute-start.9 = (bf16[64,1768]{1,0:T(8,128)(2,1)S(1)}, bf16[64,1768]{1,0:T(8,128)(2,1)S(1)}, u32[]{:S(2)}, u32[]{:S(2)}) collective-permute-start(bf16[64,1768]{1,0:T(8,128)(2,1)S(1)} %constant_dynamic-update-slice_fusion.2.refs_4_), channel_id=1, source_target_pairs={{0,4},{1,3},{4,8},{5,1},{8,12},{9,5},{12,14},{13,9},{14,10},{15,13... | collective-permute-start | bytes 678920 | tf_op jit(solution)/shard_map/ppermute | solution.py:54
  14.7 13.9 %copy-start.2 = (bf16[64,1768]{1,0:T(8,128)(2,1)}, bf16[64,1768]{1,0:T(8,128)(2,1)S(1)}, u32[]{:S(2)}) copy-start(bf16[64,1768]{1,0:T(8,128)(2,1)S(1)} %collective-permute-done.8.refs_7_) | copy-start | bytes 678916
  14.7 6.4 %collective-permute-start.12 = (bf16[64,1768]{1,0:T(8,128)(2,1)S(1)}, bf16[64,1768]{1,0:T(8,128)(2,1)S(1)}, u32[]{:S(2)}, u32[]{:S(2)}) collective-permute-start(bf16[64,1768]{1,0:T(8,128)(2,1)S(1)} %collective-permute-done.8.refs_7_), channel_id=1, source_target_pairs={{0,4},{1,3},{4,8},{5,1},{8,12},{9,5},{12,14},{13,9},{14,10},{15,13... | collective-permute-start | bytes 678920 | tf_op jit(solution)/shard_map/ppermute | solution.py:54
  16.3 1.5 %collective-permute-start = (bf16[64,768]{1,0:T(8,128)(2,1)}, bf16[64,768]{1,0:T(8,128)(2,1)S(1)}, u32[]{:S(2)}, u32[]{:S(2)}) collective-permute-start(bf16[64,768]{1,0:T(8,128)(2,1)} %param.4), channel_id=1, source_target_pairs={{0,1},{1,0},{4,5},{5,4},{8,9},{9,8},{12,13},{13,12},{14,15},{15,14... | collective-permute-start | bytes 294920 | tf_op jit(solution)/shard_map/ppermute | solution.py:54
  16.3 7.7 %collective-permute-start.1 = (bf16[64,1000]{1,0:T(8,128)(2,1)}, bf16[64,1000]{1,0:T(8,128)(2,1)S(1)}, u32[]{:S(2)}, u32[]{:S(2)}) collective-permute-start(bf16[64,1000]{1,0:T(8,128)(2,1)} %param.5), channel_id=1, source_target_pairs={{0,1},{1,0},{4,5},{5,4},{8,9},{9,8},{12,13},{13,12},{14,15},{15,14... | collective-permute-start | bytes 384008 | tf_op jit(solution)/shard_map/ppermute | solution.py:54
  16.8 7.2 %collective-permute-start.6 = (bf16[64,1768]{1,0:T(8,128)(2,1)S(1)}, bf16[64,1768]{1,0:T(8,128)(2,1)S(1)}, u32[]{:S(2)}, u32[]{:S(2)}) collective-permute-start(bf16[64,1768]{1,0:T(8,128)(2,1)S(1)} %constant_dynamic-update-slice_fusion.refs_3_), channel_id=1, source_target_pairs={{0,1},{1,0},{4,5},{5,4},{8,9},{9,8},{12,13},{13,12},{14,15},{15,14... | collective-permute-start | bytes 678920 | tf_op jit(solution)/shard_map/ppermute | solution.py:54
  17.8 6.7 %collective-permute-start.7 = (bf16[64,1768]{1,0:T(8,128)(2,1)S(1)}, bf16[64,1768]{1,0:T(8,128)(2,1)S(1)}, u32[]{:S(2)}, u32[]{:S(2)}) collective-permute-start(bf16[64,1768]{1,0:T(8,128)(2,1)S(1)} %constant_dynamic-update-slice_fusion.2.refs_4_), channel_id=1, source_target_pairs={{0,1},{1,0},{4,5},{5,4},{8,9},{9,8},{12,13},{13,12},{14,15},{15,14... | collective-permute-start | bytes 678920 | tf_op jit(solution)/shard_map/ppermute | solution.py:54
  17.9 10.7 %copy-start.3 = (bf16[64,1768]{1,0:T(8,128)(2,1)}, bf16[64,1768]{1,0:T(8,128)(2,1)S(1)}, u32[]{:S(2)}) copy-start(bf16[64,1768]{1,0:T(8,128)(2,1)S(1)} %collective-permute-done.9.refs_8_) | copy-start | bytes 678916
  18.0 6.6 %collective-permute-start.13 = (bf16[64,1768]{1,0:T(8,128)(2,1)S(1)}, bf16[64,1768]{1,0:T(8,128)(2,1)S(1)}, u32[]{:S(2)}, u32[]{:S(2)}) collective-permute-start(bf16[64,1768]{1,0:T(8,128)(2,1)S(1)} %collective-permute-done.9.refs_8_), channel_id=1, source_target_pairs={{0,4},{1,3},{4,8},{5,1},{8,12},{9,5},{12,14},{13,9},{14,10},{15,13... | collective-permute-start | bytes 678920 | tf_op jit(solution)/shard_map/ppermute | solution.py:54
  21.1 7.5 %copy-start.4 = (bf16[64,1768]{1,0:T(8,128)(2,1)}, bf16[64,1768]{1,0:T(8,128)(2,1)S(1)}, u32[]{:S(2)}) copy-start(bf16[64,1768]{1,0:T(8,128)(2,1)S(1)} %collective-permute-done.12.refs_11_) | copy-start | bytes 678916
  21.1 6.0 %collective-permute-start.16 = (bf16[64,1768]{1,0:T(8,128)(2,1)S(1)}, bf16[64,1768]{1,0:T(8,128)(2,1)S(1)}, u32[]{:S(2)}, u32[]{:S(2)}) collective-permute-start(bf16[64,1768]{1,0:T(8,128)(2,1)S(1)} %collective-permute-done.12.refs_11_), channel_id=1, source_target_pairs={{0,4},{1,3},{4,8},{5,1},{8,12},{9,5},{12,14},{13,9},{14,10},{15,13... | collective-permute-start | bytes 678920 | tf_op jit(solution)/shard_map/ppermute | solution.py:54
  24.0 3.9 %collective-permute-start.10 = (bf16[64,1768]{1,0:T(8,128)(2,1)S(1)}, bf16[64,1768]{1,0:T(8,128)(2,1)S(1)}, u32[]{:S(2)}, u32[]{:S(2)}) collective-permute-start(bf16[64,1768]{1,0:T(8,128)(2,1)S(1)} %collective-permute-done.8.refs_7_), channel_id=1, source_target_pairs={{0,1},{1,0},{4,5},{5,4},{8,9},{9,8},{12,13},{13,12},{14,15},{15,14... | collective-permute-start | bytes 678920 | tf_op jit(solution)/shard_map/ppermute | solution.py:54
  24.0 4.7 %copy-start.5 = (bf16[64,1768]{1,0:T(8,128)(2,1)}, bf16[64,1768]{1,0:T(8,128)(2,1)S(1)}, u32[]{:S(2)}) copy-start(bf16[64,1768]{1,0:T(8,128)(2,1)S(1)} %collective-permute-done.6.refs_5_) | copy-start | bytes 678916
  24.0 3.9 %collective-permute-start.11 = (bf16[64,1768]{1,0:T(8,128)(2,1)S(1)}, bf16[64,1768]{1,0:T(8,128)(2,1)S(1)}, u32[]{:S(2)}, u32[]{:S(2)}) collective-permute-start(bf16[64,1768]{1,0:T(8,128)(2,1)S(1)} %collective-permute-done.9.refs_8_), channel_id=1, source_target_pairs={{0,1},{1,0},{4,5},{5,4},{8,9},{9,8},{12,13},{13,12},{14,15},{15,14... | collective-permute-start | bytes 678920 | tf_op jit(solution)/shard_map/ppermute | solution.py:54
  24.5 3.4 %collective-permute-start.14 = (bf16[64,1768]{1,0:T(8,128)(2,1)S(1)}, bf16[64,1768]{1,0:T(8,128)(2,1)S(1)}, u32[]{:S(2)}, u32[]{:S(2)}) collective-permute-start(bf16[64,1768]{1,0:T(8,128)(2,1)S(1)} %collective-permute-done.12.refs_11_), channel_id=1, source_target_pairs={{0,1},{1,0},{4,5},{5,4},{8,9},{9,8},{12,13},{13,12},{14,15},{15,14... | collective-permute-start | bytes 678920 | tf_op jit(solution)/shard_map/ppermute | solution.py:54
  24.6 3.3 %collective-permute-start.15 = (bf16[64,1768]{1,0:T(8,128)(2,1)S(1)}, bf16[64,1768]{1,0:T(8,128)(2,1)S(1)}, u32[]{:S(2)}, u32[]{:S(2)}) collective-permute-start(bf16[64,1768]{1,0:T(8,128)(2,1)S(1)} %collective-permute-done.13.refs_12_), channel_id=1, source_target_pairs={{0,1},{1,0},{4,5},{5,4},{8,9},{9,8},{12,13},{13,12},{14,15},{15,14... | collective-permute-start | bytes 678920 | tf_op jit(solution)/shard_map/ppermute | solution.py:54
  27.1 1.5 %collective-permute-start.17 = (bf16[64,1768]{1,0:T(8,128)(2,1)S(1)}, bf16[64,1768]{1,0:T(8,128)(2,1)S(1)}, u32[]{:S(2)}, u32[]{:S(2)}) collective-permute-start(bf16[64,1768]{1,0:T(8,128)(2,1)S(1)} %collective-permute-done.16.refs_15_), channel_id=1, source_target_pairs={{0,1},{1,0},{4,5},{5,4},{8,9},{9,8},{12,13},{13,12},{14,15},{15,14... | collective-permute-start | bytes 678920 | tf_op jit(solution)/shard_map/ppermute | solution.py:54
  (8 other events, 13.8 us)

commit v2 on v1

v2 whole, which is shorter than its diff:
```python
import functools

import jax
import jax.numpy as jnp
from jax import lax
from jax.experimental import pallas as pl
from jax.experimental.pallas import tpu as pltpu
from jax.sharding import PartitionSpec as P

AXES = ("blk", "pair")
F32, BF16 = jnp.float32, jnp.bfloat16
WHOLE = pl.BlockSpec(memory_space=pltpu.VMEM)
PARAMS = pltpu.CompilerParams(vmem_limit_bytes=28 * 2**20)


def ring_of(chips):
    if chips == 8:
        return [0, 2, 4, 6, 7, 5, 3, 1]
    return list(range(chips))


def hop(ring, shift):
    n, out = len(ring), []
    for place, chip in enumerate(ring):
        for core, step in ((0, shift), (1, -shift)):
            out.append((chip * 2 + core, ring[(place + step) % n] * 2 + 1 - core))
    return out


def begin(q_hbm, k_hbm, l_hbm, top_ref, totals_ref, weighted_ref, q_ref, own_ref, q_in, k_in, l_in, sem):
    copies = [
        pltpu.make_async_copy(source, target, sem.at[n])
        for n, (source, target) in enumerate([(k_hbm, k_in), (l_hbm, l_in), (q_hbm, q_in)])
    ]
    for copy in copies:
        copy.start()
    for copy in copies:
        copy.wait()
    keys, labels, q = k_in[...], l_in[...], q_in[...].T
    width = keys.shape[1]
    own_ref[:, :width] = keys
    own_ref[:, width:] = labels
    q_ref[...] = q
    scores = jnp.dot(keys, q, preferred_element_type=F32) * width**-0.5
    top = jnp.max(scores, axis=0, keepdims=True)
    weights = jnp.exp(scores - top)
    top_ref[...] = top
    totals_ref[...] = jnp.sum(weights, axis=0, keepdims=True)
    weighted_ref[...] = jnp.dot(labels.T, weights.astype(BF16), preferred_element_type=F32)


def begin_call(queries, key_rows, label_rows):
    (rows, width), (count, classes) = queries.shape, label_rows.shape
    row = jax.ShapeDtypeStruct((1, rows), F32)
    operands = [pltpu.with_memory_space_constraint(x, pltpu.HBM) for x in (queries, key_rows, label_rows)]
    return pl.pallas_call(
        begin,
        out_shape=[
            row,
            row,
            jax.ShapeDtypeStruct((classes, rows), F32),
            jax.ShapeDtypeStruct((width, rows), BF16),
            jax.ShapeDtypeStruct((count, width + classes), BF16),
        ],
        in_specs=[pl.BlockSpec(memory_space=pltpu.HBM)] * 3,
        out_specs=[WHOLE] * 5,
        scratch_shapes=[
            pltpu.VMEM((rows, width), BF16),
            pltpu.VMEM((count, width), BF16),
            pltpu.VMEM((count, classes), BF16),
            pltpu.SemaphoreType.DMA((3,)),
        ],
        compiler_params=PARAMS,
    )(*operands)


def absorb(width, count, last, *refs):
    q_ref, pieces, (old_top, old_totals, old_weighted) = refs[0], refs[1 : 1 + count], refs[1 + count : 4 + count]
    refs = refs[4 + count :]
    keys = jnp.concatenate([p[:, :width] for p in pieces], axis=0)
    labels = jnp.concatenate([p[:, width:] for p in pieces], axis=0).T
    scores = jnp.dot(keys, q_ref[...], preferred_element_type=F32) * width**-0.5
    top = jnp.maximum(old_top[...], jnp.max(scores, axis=0, keepdims=True))
    factor = jnp.exp(old_top[...] - top)
    weights = jnp.exp(scores - top)
    totals = jnp.sum(weights, axis=0, keepdims=True) + old_totals[...] * factor
    weights = weights.astype(BF16)
    if not last:
        refs[0][...], refs[1][...] = top, totals
        refs[2][...] = jnp.dot(labels, weights, preferred_element_type=F32) + old_weighted[...] * factor
        return
    out_ref, done_ref, sem = refs
    rows, copies = weights.shape[1], []
    middle = rows // 256 * 128
    for n, (low, high) in enumerate([(0, middle), (middle, rows)]):
        weighted = jnp.dot(labels, weights[:, low:high], preferred_element_type=F32)
        weighted += old_weighted[:, low:high] * factor[:, low:high]
        done_ref[:, low:high] = (weighted / totals[:, low:high]).astype(BF16)
        copies.append(pltpu.make_async_copy(done_ref.at[:, low:high], out_ref.at[:, low:high], sem.at[n]))
        copies[-1].start()
    for copy in copies:
        copy.wait()


def absorb_call(q, pieces, state, last):
    (width, rows), classes = q.shape, state[2].shape[0]
    if last:
        shapes = [jax.ShapeDtypeStruct((classes, rows), BF16)]
        places = [pl.BlockSpec(memory_space=pl.ANY)]
        scratch = [pltpu.VMEM((classes, rows), BF16), pltpu.SemaphoreType.DMA((2,))]
    else:
        shapes, places, scratch = [jax.ShapeDtypeStruct(s.shape, F32) for s in state], [WHOLE] * 3, []
    operands = (q, *pieces, *state)
    return pl.pallas_call(
        functools.partial(absorb, width, len(pieces), last),
        out_shape=shapes,
        in_specs=[WHOLE] * len(operands),
        out_specs=places,
        scratch_shapes=scratch,
        compiler_params=PARAMS,
    )(*operands)


def on_device(queries, key_rows, label_rows, chips):
    half, ring = chips // 2, ring_of(chips)
    ways = hop(ring, -1), hop(ring, 1)
    cores = [(2 * chip + core, 2 * chip + 1 - core) for chip in ring for core in range(2)]

    def send(x, pairs):
        return lax.ppermute(x, AXES, pairs)

    x = jnp.concatenate([send(key_rows, ways[0]), send(label_rows, ways[0])], axis=1)
    *state, q, own = begin_call(queries, key_rows, label_rows)
    y = send(own, ways[1])
    pieces = {1: [send(own, cores)]}
    absorbed = 0

    def absorb_to(step):
        nonlocal state, absorbed
        while absorbed < step:
            absorbed += 1
            state = absorb_call(q, pieces[absorbed], state, absorbed == half)

    for step in range(1, half + 1):
        pieces.setdefault(step, [])
        if step < half:
            x_next = send(x, ways[step % 2])
        else:
            absorb_to(half - 2)
            x, state = lax.optimization_barrier((x, state))
        pieces[step] += [x, send(x, cores)]
        if step < half:
            pieces[step] += [y, send(y, cores)]
            if step < half - 1:
                y = send(y, ways[1 - step % 2])
            x = x_next
    absorb_to(half)
    return state[0].T


def solution(mesh):
    chips = mesh.shape["blk"]
    spec = P(("parts", "blk", "pair"), None)
    return jax.shard_map(
        lambda q, k, l: on_device(q, k, l, chips),
        mesh=mesh,
        in_specs=(spec, spec, spec),
        out_specs=spec,
        check_vma=False,
    )
```

time: 40.8 us -> 29 us (0.71)
  waiting for transfers between devices: 10.2 us -> 2.69 us
  other arithmetic: 2.42 us -> 0 us
  Pallas kernels: 11 us -> 9.9 us
  local copies, waits for them, and re-layouts: 0.87 us -> 0.02 us
    ppermute x18 -> x16, waiting for transfers between devices: 10.2 us -> 2.69 us  [send(): return lax.ppermute(x, AXES, pairs)]
    concatenate x2 -> x0, other arithmetic: 2.42 us -> none  [beside(): return jnp.concatenate([k, l], axis=1)]
    pallas_call x1 -> x5, Pallas kernels: 11 us -> 9.9 us  [the longest x4 7.3 us: absorb_call(): pl.pallas_call(functools.partial(absorb, width, len(pieces), last), out_s...]
    unnamed x30 -> x1, local copies, waits for them, and re-layouts: 0.85 us -> 0.01 us
    ppermute x18 -> x16, starting transfers between devices: 15.8 us -> 16.2 us  [send(): return lax.ppermute(x, AXES, pairs)]
  transfers between devices with their start and end apart: 18 -> 16, of which waited for: 7 -> 2; matrix products, arithmetic and copies ran while one was open for 6% -> 0% of each run, Pallas kernels for 0% -> 27%
where the time goes in v2:
time: 29 us; the launch traced here: 28.9 us
  starting transfers between devices  16.2 us (56%)
  Pallas kernels  9.9 us (34%)
  waiting for transfers between devices  2.69 us (9%)
    ppermute x16, starting transfers between devices, send(): return lax.ppermute(x, AXES, pairs)  16.2 us
    pallas_call x4, Pallas kernels, absorb_call(): pl.pallas_call(functools.partial(absorb, width, len(pieces), last), out_s...  7.3 us
    ppermute x16, waiting for transfers between devices, send(): return lax.ppermute(x, AXES, pairs)  2.69 us
    pallas_call x1, Pallas kernels, begin_call(): pl.pallas_call(begin, out_shape=[row, row, jax.ShapeDtypeStruct((classes,...  2.6 us
  transfers between devices with their start and end apart: 16, of which 2 were waited for; matrix products, arithmetic and copies ran while one was open for 0% of the time, Pallas kernels for 27%

profile of v2, /device:TPU:0, one launch (start us, length us, event | category | flops | bytes accessed | tf_op | source)
XLA Modules:
  0.0 28.9 jit_solution(6536260936068038683)
XLA Ops:
  0.0 2.4 %collective-permute-start = (bf16[64,768]{1,0:T(8,128)(2,1)}, bf16[64,768]{1,0:T(8,128)(2,1)S(1)}, u32[]{:S(2)}, u32[]{:S(2)}) collective-permute-start(bf16[64,768]{1,0:T(8,128)(2,1)} %k_hbm.1), channel_id=1, source_target_pairs={{0,3},{1,4},{4,1},{5,8},{8,5},{9,12},{12,9},{13,14},{14,13},{15,10... | collective-permute-start | bytes 294920 | tf_op jit(solution)/shard_map/ppermute | solution.py:130
  2.4 0.0 collective-permute-start.1
  2.4 2.6 %shard_map.37 = (f32[1,896]{1,0:T(1,128)S(1)}, f32[1,896]{1,0:T(1,128)S(1)}, f32[1000,896]{1,0:T(8,128)S(1)}, bf16[768,896]{1,0:T(8,128)(2,1)S(1)}, bf16[64,1768]{1,0:T(8,128)(2,1)S(1)}) custom-call(bf16[896,768]{1,0:T(8,128)(2,1)} %q_hbm.1, bf16[64,768]{1,0:T(8,128)(2,1)} %k_hbm.1, bf16[64,1000]{1,0:T(8,128)(2,1)} %l_hbm.1), custom_call_target="tpu_custom_call" | custom-call | tf_op jit(solution)/shard_map/pallas_call | solution.py:56
  5.1 2.0 %collective-permute-start.6 = (bf16[64,1768]{1,0:T(8,128)(2,1)S(1)}, bf16[64,1768]{1,0:T(8,128)(2,1)S(1)}, u32[]{:S(2)}, u32[]{:S(2)}) collective-permute-start(bf16[64,1768]{1,0:T(8,128)(2,1)S(1)} %get-tuple-element.24), channel_id=1, source_target_pairs={{0,5},{1,2},{4,9},{5,0},{8,13},{9,4},{12,15},{13,8},{14,11},{15,12... | collective-permute-start | bytes 678920 | tf_op jit(solution)/shard_map/ppermute | solution.py:130
  7.0 0.0 collective-permute-done.1
  7.1 1.9 %collective-permute-start.2 = (bf16[64,1768]{1,0:T(8,128)(2,1)S(1)}, bf16[64,1768]{1,0:T(8,128)(2,1)S(1)}, u32[]{:S(2)}, u32[]{:S(2)}) collective-permute-start(bf16[64,1768]{1,0:T(8,128)(2,1)S(1)} %constant_dynamic-update-slice_fusion.refs_2_), channel_id=1, source_target_pairs={{0,5},{1,2},{4,9},{5,0},{8,13},{9,4},{12,15},{13,8},{14,11},{15,12... | collective-permute-start | bytes 678920 | tf_op jit(solution)/shard_map/ppermute | solution.py:130
  9.0 1.7 %collective-permute-done.6.refs_4_ = bf16[64,1768]{1,0:T(8,128)(2,1)S(1)} collective-permute-done((bf16[64,1768]{1,0:T(8,128)(2,1)S(1)}, bf16[64,1768]{1,0:T(8,128)(2,1)S(1)}, u32[]{:S(2)}, u32[]{:S(2)}) %collective-permute-start.6) | collective-permute-done | bytes 226336 | tf_op jit(solution)/shard_map/ppermute | solution.py:130
  10.7 1.9 %collective-permute-start.7 = (bf16[64,1768]{1,0:T(8,128)(2,1)S(1)}, bf16[64,1768]{1,0:T(8,128)(2,1)S(1)}, u32[]{:S(2)}, u32[]{:S(2)}) collective-permute-start(bf16[64,1768]{1,0:T(8,128)(2,1)S(1)} %collective-permute-done.6.refs_4_), channel_id=1, source_target_pairs={{0,3},{1,4},{4,1},{5,8},{8,5},{9,12},{12,9},{13,14},{14,13},{15,10... | collective-permute-start | bytes 678920 | tf_op jit(solution)/shard_map/ppermute | solution.py:130
  12.7 0.3 %collective-permute-start.9 = (bf16[64,1768]{1,0:T(8,128)(2,1)S(1)}, bf16[64,1768]{1,0:T(8,128)(2,1)S(1)}, u32[]{:S(2)}, u32[]{:S(2)}) collective-permute-start(bf16[64,1768]{1,0:T(8,128)(2,1)S(1)} %get-tuple-element.24), channel_id=1, source_target_pairs={{0,1},{1,0},{4,5},{5,4},{8,9},{9,8},{12,13},{13,12},{14,15},{15,14... | collective-permute-start | bytes 678920 | tf_op jit(solution)/shard_map/ppermute | solution.py:130
  13.0 0.2 collective-permute-start.10
  13.2 0.0 collective-permute-done.2.refs_1_
  13.2 1.8 %collective-permute-start.3 = (bf16[64,1768]{1,0:T(8,128)(2,1)S(1)}, bf16[64,1768]{1,0:T(8,128)(2,1)S(1)}, u32[]{:S(2)}, u32[]{:S(2)}) collective-permute-start(bf16[64,1768]{1,0:T(8,128)(2,1)S(1)} %collective-permute-done.2.refs_1_), channel_id=1, source_target_pairs={{0,3},{1,4},{4,1},{5,8},{8,5},{9,12},{12,9},{13,14},{14,13},{15,10... | collective-permute-start | bytes 678920 | tf_op jit(solution)/shard_map/ppermute | solution.py:130
  15.0 0.5 %collective-permute-start.11 = (bf16[64,1768]{1,0:T(8,128)(2,1)S(1)}, bf16[64,1768]{1,0:T(8,128)(2,1)S(1)}, u32[]{:S(2)}, u32[]{:S(2)}) collective-permute-start(bf16[64,1768]{1,0:T(8,128)(2,1)S(1)} %collective-permute-done.6.refs_4_), channel_id=1, source_target_pairs={{0,1},{1,0},{4,5},{5,4},{8,9},{9,8},{12,13},{13,12},{14,15},{15,14... | collective-permute-start | bytes 678920 | tf_op jit(solution)/shard_map/ppermute | solution.py:130
  15.5 0.9 %collective-permute-done.7.refs_3_ = bf16[64,1768]{1,0:T(8,128)(2,1)S(1)} collective-permute-done((bf16[64,1768]{1,0:T(8,128)(2,1)S(1)}, bf16[64,1768]{1,0:T(8,128)(2,1)S(1)}, u32[]{:S(2)}, u32[]{:S(2)}) %collective-permute-start.7) | collective-permute-done | bytes 226336 | tf_op jit(solution)/shard_map/ppermute | solution.py:130
  16.4 2.1 %collective-permute-start.14 = (bf16[64,1768]{1,0:T(8,128)(2,1)S(1)}, bf16[64,1768]{1,0:T(8,128)(2,1)S(1)}, u32[]{:S(2)}, u32[]{:S(2)}) collective-permute-start(bf16[64,1768]{1,0:T(8,128)(2,1)S(1)} %collective-permute-done.7.refs_3_), channel_id=1, source_target_pairs={{0,5},{1,2},{4,9},{5,0},{8,13},{9,4},{12,15},{13,8},{14,11},{15,12... | collective-permute-start | bytes 678920 | tf_op jit(solution)/shard_map/ppermute | solution.py:130
  18.5 0.5 %collective-permute-start.8 = (bf16[64,1768]{1,0:T(8,128)(2,1)S(1)}, bf16[64,1768]{1,0:T(8,128)(2,1)S(1)}, u32[]{:S(2)}, u32[]{:S(2)}) collective-permute-start(bf16[64,1768]{1,0:T(8,128)(2,1)S(1)} %collective-permute-done.7.refs_3_), channel_id=1, source_target_pairs={{0,1},{1,0},{4,5},{5,4},{8,9},{9,8},{12,13},{13,12},{14,15},{15,14... | collective-permute-start | bytes 678920 | tf_op jit(solution)/shard_map/ppermute | solution.py:130
  19.0 1.6 %collective-permute-start.4 = (bf16[64,1768]{1,0:T(8,128)(2,1)S(1)}, bf16[64,1768]{1,0:T(8,128)(2,1)S(1)}, u32[]{:S(2)}, u32[]{:S(2)}) collective-permute-start(bf16[64,1768]{1,0:T(8,128)(2,1)S(1)} %collective-permute-done.3.refs_1_), channel_id=1, source_target_pairs={{0,5},{1,2},{4,9},{5,0},{8,13},{9,4},{12,15},{13,8},{14,11},{15,12... | collective-permute-start | bytes 678920 | tf_op jit(solution)/shard_map/ppermute | solution.py:130
  20.7 2.2 %shard_map.38 = (f32[1,896]{1,0:T(1,128)S(1)}, f32[1,896]{1,0:T(1,128)S(1)}, f32[1000,896]{1,0:T(8,128)S(1)}) custom-call(bf16[768,896]{1,0:T(8,128)(2,1)S(1)} %get-tuple-element.23.refs_0_, bf16[64,1768]{1,0:T(8,128)(2,1)S(1)} %collective-permute-done.9.refs_1_, bf16[64,1768]{1,0:T(8,128)(2,1)S(1)} %constant_dynamic-update-slice_fusion.refs_2_, ...), custom_call_target="tpu_custom_call" | custom-call | tf_op jit(solution)/shard_map/pallas_call | solution.py:114
  22.9 0.2 collective-permute-start.13
  23.1 0.3 %collective-permute-start.15 = (bf16[64,1768]{1,0:T(8,128)(2,1)S(1)}, bf16[64,1768]{1,0:T(8,128)(2,1)S(1)}, u32[]{:S(2)}, u32[]{:S(2)}) collective-permute-start(bf16[64,1768]{1,0:T(8,128)(2,1)S(1)} %collective-permute-done.14.refs_3_), channel_id=1, source_target_pairs={{0,1},{1,0},{4,5},{5,4},{8,9},{9,8},{12,13},{13,12},{14,15},{15,14... | collective-permute-start | bytes 678920 | tf_op jit(solution)/shard_map/ppermute | solution.py:130
  23.5 1.5 %shard_map.39 = (f32[1,896]{1,0:T(1,128)S(1)}, f32[1,896]{1,0:T(1,128)S(1)}, f32[1000,896]{1,0:T(8,128)S(1)}) custom-call(bf16[768,896]{1,0:T(8,128)(2,1)S(1)} %get-tuple-element.23.refs_0_, bf16[64,1768]{1,0:T(8,128)(2,1)S(1)} %collective-permute-done.2.refs_1_, bf16[64,1768]{1,0:T(8,128)(2,1)S(1)} %collective-permute-done.5.refs_2_, ...), custom_call_target="tpu_custom_call" | custom-call | tf_op jit(solution)/shard_map/pallas_call | solution.py:114
  25.0 0.3 collective-permute-start.12
  25.2 1.5 %shard_map.40 = (f32[1,896]{1,0:T(1,128)S(1)}, f32[1,896]{1,0:T(1,128)S(1)}, f32[1000,896]{1,0:T(8,128)S(1)}) custom-call(bf16[768,896]{1,0:T(8,128)(2,1)S(1)} %get-tuple-element.23.refs_0_, bf16[64,1768]{1,0:T(8,128)(2,1)S(1)} %collective-permute-done.3.refs_1_, bf16[64,1768]{1,0:T(8,128)(2,1)S(1)} %collective-permute-done.13.refs_2_, ...), custom_call_target="tpu_custom_call" | custom-call | tf_op jit(solution)/shard_map/pallas_call | solution.py:114
  26.8 2.1 %shard_map.41 = bf16[1000,896]{1,0:T(8,128)(2,1)} custom-call(bf16[768,896]{1,0:T(8,128)(2,1)S(1)} %get-tuple-element.23.refs_0_, bf16[64,1768]{1,0:T(8,128)(2,1)S(1)} %collective-permute-done.4.refs_1_, bf16[64,1768]{1,0:T(8,128)(2,1)S(1)} %collective-permute-done.12.refs_2_, f32[1,896]{1,0:T(1,128)S(1)} %get-tuple-element.38.refs_3_, ...), custom_call_target="tpu_custom_call" | custom-call | tf_op jit(solution)/shard_map/pallas_call | solution.py:114
  (15 shorter events, 0.1 us)
Async XLA Ops:
  0.0 7.0 %collective-permute-start = (bf16[64,768]{1,0:T(8,128)(2,1)}, bf16[64,768]{1,0:T(8,128)(2,1)S(1)}, u32[]{:S(2)}, u32[]{:S(2)}) collective-permute-start(bf16[64,768]{1,0:T(8,128)(2,1)} %k_hbm.1), channel_id=1, source_target_pairs={{0,3},{1,4},{4,1},{5,8},{8,5},{9,12},{12,9},{13,14},{14,13},{15,10... | collective-permute-start | bytes 294920 | tf_op jit(solution)/shard_map/ppermute | solution.py:130
  2.4 4.6 %collective-permute-start.1 = (bf16[64,1000]{1,0:T(8,128)(2,1)}, bf16[64,1000]{1,0:T(8,128)(2,1)S(1)}, u32[]{:S(2)}, u32[]{:S(2)}) collective-permute-start(bf16[64,1000]{1,0:T(8,128)(2,1)} %l_hbm.1), channel_id=1, source_target_pairs={{0,3},{1,4},{4,1},{5,8},{8,5},{9,12},{12,9},{13,14},{14,13},{15,10... | collective-permute-start | bytes 384008 | tf_op jit(solution)/shard_map/ppermute | solution.py:130
  5.1 5.7 %collective-permute-start.6 = (bf16[64,1768]{1,0:T(8,128)(2,1)S(1)}, bf16[64,1768]{1,0:T(8,128)(2,1)S(1)}, u32[]{:S(2)}, u32[]{:S(2)}) collective-permute-start(bf16[64,1768]{1,0:T(8,128)(2,1)S(1)} %get-tuple-element.24), channel_id=1, source_target_pairs={{0,5},{1,2},{4,9},{5,0},{8,13},{9,4},{12,15},{13,8},{14,11},{15,12... | collective-permute-start | bytes 678920 | tf_op jit(solution)/shard_map/ppermute | solution.py:130
  7.1 6.1 %collective-permute-start.2 = (bf16[64,1768]{1,0:T(8,128)(2,1)S(1)}, bf16[64,1768]{1,0:T(8,128)(2,1)S(1)}, u32[]{:S(2)}, u32[]{:S(2)}) collective-permute-start(bf16[64,1768]{1,0:T(8,128)(2,1)S(1)} %constant_dynamic-update-slice_fusion.refs_2_), channel_id=1, source_target_pairs={{0,5},{1,2},{4,9},{5,0},{8,13},{9,4},{12,15},{13,8},{14,11},{15,12... | collective-permute-start | bytes 678920 | tf_op jit(solution)/shard_map/ppermute | solution.py:130
  10.7 5.7 %collective-permute-start.7 = (bf16[64,1768]{1,0:T(8,128)(2,1)S(1)}, bf16[64,1768]{1,0:T(8,128)(2,1)S(1)}, u32[]{:S(2)}, u32[]{:S(2)}) collective-permute-start(bf16[64,1768]{1,0:T(8,128)(2,1)S(1)} %collective-permute-done.6.refs_4_), channel_id=1, source_target_pairs={{0,3},{1,4},{4,1},{5,8},{8,5},{9,12},{12,9},{13,14},{14,13},{15,10... | collective-permute-start | bytes 678920 | tf_op jit(solution)/shard_map/ppermute | solution.py:130
  12.7 5.8 %collective-permute-start.9 = (bf16[64,1768]{1,0:T(8,128)(2,1)S(1)}, bf16[64,1768]{1,0:T(8,128)(2,1)S(1)}, u32[]{:S(2)}, u32[]{:S(2)}) collective-permute-start(bf16[64,1768]{1,0:T(8,128)(2,1)S(1)} %get-tuple-element.24), channel_id=1, source_target_pairs={{0,1},{1,0},{4,5},{5,4},{8,9},{9,8},{12,13},{13,12},{14,15},{15,14... | collective-permute-start | bytes 678920 | tf_op jit(solution)/shard_map/ppermute | solution.py:130
  13.0 5.5 %collective-permute-start.10 = (bf16[64,1768]{1,0:T(8,128)(2,1)S(1)}, bf16[64,1768]{1,0:T(8,128)(2,1)S(1)}, u32[]{:S(2)}, u32[]{:S(2)}) collective-permute-start(bf16[64,1768]{1,0:T(8,128)(2,1)S(1)} %constant_dynamic-update-slice_fusion.refs_2_), channel_id=1, source_target_pairs={{0,1},{1,0},{4,5},{5,4},{8,9},{9,8},{12,13},{13,12},{14,15},{15,14... | collective-permute-start | bytes 678920 | tf_op jit(solution)/shard_map/ppermute | solution.py:130
  13.2 5.8 %collective-permute-start.3 = (bf16[64,1768]{1,0:T(8,128)(2,1)S(1)}, bf16[64,1768]{1,0:T(8,128)(2,1)S(1)}, u32[]{:S(2)}, u32[]{:S(2)}) collective-permute-start(bf16[64,1768]{1,0:T(8,128)(2,1)S(1)} %collective-permute-done.2.refs_1_), channel_id=1, source_target_pairs={{0,3},{1,4},{4,1},{5,8},{8,5},{9,12},{12,9},{13,14},{14,13},{15,10... | collective-permute-start | bytes 678920 | tf_op jit(solution)/shard_map/ppermute | solution.py:130
  15.0 5.7 %collective-permute-start.11 = (bf16[64,1768]{1,0:T(8,128)(2,1)S(1)}, bf16[64,1768]{1,0:T(8,128)(2,1)S(1)}, u32[]{:S(2)}, u32[]{:S(2)}) collective-permute-start(bf16[64,1768]{1,0:T(8,128)(2,1)S(1)} %collective-permute-done.6.refs_4_), channel_id=1, source_target_pairs={{0,1},{1,0},{4,5},{5,4},{8,9},{9,8},{12,13},{13,12},{14,15},{15,14... | collective-permute-start | bytes 678920 | tf_op jit(solution)/shard_map/ppermute | solution.py:130
  16.4 6.7 %collective-permute-start.14 = (bf16[64,1768]{1,0:T(8,128)(2,1)S(1)}, bf16[64,1768]{1,0:T(8,128)(2,1)S(1)}, u32[]{:S(2)}, u32[]{:S(2)}) collective-permute-start(bf16[64,1768]{1,0:T(8,128)(2,1)S(1)} %collective-permute-done.7.refs_3_), channel_id=1, source_target_pairs={{0,5},{1,2},{4,9},{5,0},{8,13},{9,4},{12,15},{13,8},{14,11},{15,12... | collective-permute-start | bytes 678920 | tf_op jit(solution)/shard_map/ppermute | solution.py:130
  18.5 4.9 %collective-permute-start.5 = (bf16[64,1768]{1,0:T(8,128)(2,1)S(1)}, bf16[64,1768]{1,0:T(8,128)(2,1)S(1)}, u32[]{:S(2)}, u32[]{:S(2)}) collective-permute-start(bf16[64,1768]{1,0:T(8,128)(2,1)S(1)} %collective-permute-done.2.refs_1_), channel_id=1, source_target_pairs={{0,1},{1,0},{4,5},{5,4},{8,9},{9,8},{12,13},{13,12},{14,15},{15,14... | collective-permute-start | bytes 678920 | tf_op jit(solution)/shard_map/ppermute | solution.py:130
  18.5 4.9 %collective-permute-start.8 = (bf16[64,1768]{1,0:T(8,128)(2,1)S(1)}, bf16[64,1768]{1,0:T(8,128)(2,1)S(1)}, u32[]{:S(2)}, u32[]{:S(2)}) collective-permute-start(bf16[64,1768]{1,0:T(8,128)(2,1)S(1)} %collective-permute-done.7.refs_3_), channel_id=1, source_target_pairs={{0,1},{1,0},{4,5},{5,4},{8,9},{9,8},{12,13},{13,12},{14,15},{15,14... | collective-permute-start | bytes 678920 | tf_op jit(solution)/shard_map/ppermute | solution.py:130
  19.0 5.9 %collective-permute-start.4 = (bf16[64,1768]{1,0:T(8,128)(2,1)S(1)}, bf16[64,1768]{1,0:T(8,128)(2,1)S(1)}, u32[]{:S(2)}, u32[]{:S(2)}) collective-permute-start(bf16[64,1768]{1,0:T(8,128)(2,1)S(1)} %collective-permute-done.3.refs_1_), channel_id=1, source_target_pairs={{0,5},{1,2},{4,9},{5,0},{8,13},{9,4},{12,15},{13,8},{14,11},{15,12... | collective-permute-start | bytes 678920 | tf_op jit(solution)/shard_map/ppermute | solution.py:130
  22.9 2.4 %collective-permute-start.13 = (bf16[64,1768]{1,0:T(8,128)(2,1)S(1)}, bf16[64,1768]{1,0:T(8,128)(2,1)S(1)}, u32[]{:S(2)}, u32[]{:S(2)}) collective-permute-start(bf16[64,1768]{1,0:T(8,128)(2,1)S(1)} %collective-permute-done.3.refs_1_), channel_id=1, source_target_pairs={{0,1},{1,0},{4,5},{5,4},{8,9},{9,8},{12,13},{13,12},{14,15},{15,14... | collective-permute-start | bytes 678920 | tf_op jit(solution)/shard_map/ppermute | solution.py:130
  23.1 2.1 %collective-permute-start.15 = (bf16[64,1768]{1,0:T(8,128)(2,1)S(1)}, bf16[64,1768]{1,0:T(8,128)(2,1)S(1)}, u32[]{:S(2)}, u32[]{:S(2)}) collective-permute-start(bf16[64,1768]{1,0:T(8,128)(2,1)S(1)} %collective-permute-done.14.refs_3_), channel_id=1, source_target_pairs={{0,1},{1,0},{4,5},{5,4},{8,9},{9,8},{12,13},{13,12},{14,15},{15,14... | collective-permute-start | bytes 678920 | tf_op jit(solution)/shard_map/ppermute | solution.py:130
  25.0 1.8 %collective-permute-start.12 = (bf16[64,1768]{1,0:T(8,128)(2,1)S(1)}, bf16[64,1768]{1,0:T(8,128)(2,1)S(1)}, u32[]{:S(2)}, u32[]{:S(2)}) collective-permute-start(bf16[64,1768]{1,0:T(8,128)(2,1)S(1)} %collective-permute-done.4.refs_1_), channel_id=1, source_target_pairs={{0,1},{1,0},{4,5},{5,4},{8,9},{9,8},{12,13},{13,12},{14,15},{15,14... | collective-permute-start | bytes 678920 | tf_op jit(solution)/shard_map/ppermute | solution.py:130

commit v3 on v2

v3 whole, which is shorter than its diff:
```python
import functools

import jax
import jax.numpy as jnp
from jax import lax
from jax.experimental import pallas as pl
from jax.experimental.pallas import tpu as pltpu
from jax.sharding import PartitionSpec as P

AXES = ("blk", "pair")
F32, BF16 = jnp.float32, jnp.bfloat16
WHOLE = pl.BlockSpec(memory_space=pltpu.VMEM)
PARAMS = pltpu.CompilerParams(vmem_limit_bytes=28 * 2**20)


def ring_of(chips):
    if chips == 8:
        return [0, 2, 4, 6, 7, 5, 3, 1]
    return list(range(chips))


def hop(ring, shift):
    n, out = len(ring), []
    for place, chip in enumerate(ring):
        for core, step in ((0, shift), (1, -shift)):
            out.append((chip * 2 + core, ring[(place + step) % n] * 2 + 1 - core))
    return out


def begin(q_hbm, k_hbm, l_hbm, q_ref, own_ref, q_in, k_in, l_in, sem):
    copies = [
        pltpu.make_async_copy(source, target, sem.at[n])
        for n, (source, target) in enumerate([(k_hbm, k_in), (l_hbm, l_in), (q_hbm, q_in)])
    ]
    for copy in copies:
        copy.start()
    for copy in copies:
        copy.wait()
    width = k_in.shape[1]
    own_ref[:, :width] = k_in[...]
    own_ref[:, width:] = l_in[...]
    q_ref[...] = q_in[...].T


def begin_call(queries, key_rows, label_rows):
    (rows, width), (count, classes) = queries.shape, label_rows.shape
    operands = [pltpu.with_memory_space_constraint(x, pltpu.HBM) for x in (queries, key_rows, label_rows)]
    return pl.pallas_call(
        begin,
        out_shape=[
            jax.ShapeDtypeStruct((width, rows), BF16),
            jax.ShapeDtypeStruct((count, width + classes), BF16),
        ],
        in_specs=[pl.BlockSpec(memory_space=pltpu.HBM)] * 3,
        out_specs=[WHOLE] * 2,
        scratch_shapes=[
            pltpu.VMEM((rows, width), BF16),
            pltpu.VMEM((count, width), BF16),
            pltpu.VMEM((count, classes), BF16),
            pltpu.SemaphoreType.DMA((3,)),
        ],
        compiler_params=PARAMS,
    )(*operands)


def absorb(width, count, first, last, *refs):
    q_ref, pieces, refs = refs[0], refs[1 : 1 + count], refs[1 + count :]
    keys = jnp.concatenate([p[:, :width] for p in pieces], axis=0)
    labels = jnp.concatenate([p[:, width:] for p in pieces], axis=0).T
    scores = jnp.dot(keys, q_ref[...], preferred_element_type=F32) * width**-0.5
    top = jnp.max(scores, axis=0, keepdims=True)
    if not first:
        (old_top, old_totals, old_weighted), refs = refs[:3], refs[3:]
        top = jnp.maximum(old_top[...], top)
        factor = jnp.exp(old_top[...] - top)
    weights = jnp.exp(scores - top)
    totals = jnp.sum(weights, axis=0, keepdims=True)
    if not first:
        totals += old_totals[...] * factor
    weights = weights.astype(BF16)

    def weighted(low, high):
        new = jnp.dot(labels, weights[:, low:high], preferred_element_type=F32)
        return new if first else new + old_weighted[:, low:high] * factor[:, low:high]

    rows = weights.shape[1]
    if not last:
        refs[0][...], refs[1][...], refs[2][...] = top, totals, weighted(0, rows)
        return
    out_ref, done_ref, sem = refs
    copies, middle = [], rows // 256 * 128
    for n, (low, high) in enumerate([(0, middle), (middle, rows)]):
        done_ref[:, low:high] = (weighted(low, high) / totals[:, low:high]).astype(BF16)
        copies.append(pltpu.make_async_copy(done_ref.at[:, low:high], out_ref.at[:, low:high], sem.at[n]))
        copies[-1].start()
    for copy in copies:
        copy.wait()


def absorb_call(q, pieces, state, last):
    (width, rows), classes = q.shape, pieces[0].shape[1] - q.shape[0]
    if last:
        shapes = [jax.ShapeDtypeStruct((classes, rows), BF16)]
        places = [pl.BlockSpec(memory_space=pl.ANY)]
        scratch = [pltpu.VMEM((classes, rows), BF16), pltpu.SemaphoreType.DMA((2,))]
    else:
        shapes, places, scratch = [jax.ShapeDtypeStruct((n, rows), F32) for n in (1, 1, classes)], [WHOLE] * 3, []
    operands = (q, *pieces, *state)
    return pl.pallas_call(
        functools.partial(absorb, width, len(pieces), not state, last),
        out_shape=shapes,
        in_specs=[WHOLE] * len(operands),
        out_specs=places,
        scratch_shapes=scratch,
        compiler_params=PARAMS,
    )(*operands)


def on_device(queries, key_rows, label_rows, chips):
    half, ring = chips // 2, ring_of(chips)
    ways = hop(ring, -1), hop(ring, 1)
    cores = [(2 * chip + core, 2 * chip + 1 - core) for chip in ring for core in range(2)]

    def send(x, pairs):
        return lax.ppermute(x, AXES, pairs)

    x = jnp.concatenate([send(key_rows, ways[0]), send(label_rows, ways[0])], axis=1)
    q, own = begin_call(queries, key_rows, label_rows)
    y = send(own, ways[1])
    groups = [[own, send(own, cores), x]] + [[] for _ in range(half)]
    state, absorbed = (), 0

    def absorb_to(count):
        nonlocal state, absorbed
        while absorbed < count:
            state = absorb_call(q, groups[absorbed], state, absorbed == half)
            absorbed += 1

    def absorb_before(count, piece):
        nonlocal state
        absorb_to(count)
        piece, state = lax.optimization_barrier((piece, state))
        return piece

    for step in range(1, half + 1):
        if step < half:
            x_next = send(x, ways[step % 2])
            if step == 1:
                y = absorb_before(1, y)
            if step < half - 1:
                y_next = send(y, ways[1 - step % 2])
            groups[step] += [send(x, cores), y, send(y, cores)] + ([x] if step > 1 else [])
            x, y = x_next, y_next
        else:
            x = absorb_before(half - 1, x)
            groups[half] += [x, send(x, cores)]
    absorb_to(half + 1)
    return state[0].T


def solution(mesh):
    chips = mesh.shape["blk"]
    spec = P(("parts", "blk", "pair"), None)
    return jax.shard_map(
        lambda q, k, l: on_device(q, k, l, chips),
        mesh=mesh,
        in_specs=(spec, spec, spec),
        out_specs=spec,
        check_vma=False,
    )
```

time: 29 us -> 28.4 us (0.979)
  starting transfers between devices: 16.2 us -> 15.5 us
  waiting for transfers between devices: 2.69 us -> 3.26 us
  Pallas kernels: 9.9 us -> 9.39 us
    ppermute x16, starting transfers between devices: 16.2 us -> 15.5 us  [send(): return lax.ppermute(x, AXES, pairs)]
    ppermute x16, waiting for transfers between devices: 2.69 us -> 3.26 us  [send(): return lax.ppermute(x, AXES, pairs)]
    pallas_call x5 -> x6, Pallas kernels: 9.9 us -> 9.39 us  [the longest x5 7.48 us: absorb_call(): pl.pallas_call(functools.partial(absorb, width, len(pieces), not state, l...]
  transfers between devices with their start and end apart: 16 -> 16, of which waited for: 2 -> 6; matrix products, arithmetic and copies ran while one was open for 0% -> 0% of each run, Pallas kernels for 27% -> 26%
where the time goes in v3:
time: 28.4 us; the launch traced here: 28.3 us
  starting transfers between devices  15.5 us (55%)
  Pallas kernels  9.39 us (33%)
  waiting for transfers between devices  3.26 us (11%)
    ppermute x16, starting transfers between devices, send(): return lax.ppermute(x, AXES, pairs)  15.5 us
    pallas_call x5, Pallas kernels, absorb_call(): pl.pallas_call(functools.partial(absorb, width, len(pieces), not state, l...  7.48 us
    ppermute x16, waiting for transfers between devices, send(): return lax.ppermute(x, AXES, pairs)  3.26 us
    pallas_call x1, Pallas kernels, begin_call(): pl.pallas_call(begin, out_shape=[jax.ShapeDtypeStruct((width, rows), BF16...  1.91 us
  transfers between devices with their start and end apart: 16, of which 6 were waited for; matrix products, arithmetic and copies ran while one was open for 0% of the time, Pallas kernels for 26%

profile of v3, /device:TPU:0, one launch (start us, length us, event | category | flops | bytes accessed | tf_op | source)
XLA Modules:
  0.0 28.3 jit_solution(3828545857164467517)
XLA Ops:
  0.0 2.4 %collective-permute-start = (bf16[64,768]{1,0:T(8,128)(2,1)}, bf16[64,768]{1,0:T(8,128)(2,1)S(1)}, u32[]{:S(2)}, u32[]{:S(2)}) collective-permute-start(bf16[64,768]{1,0:T(8,128)(2,1)} %k_hbm.1), channel_id=1, source_target_pairs={{0,3},{1,4},{4,1},{5,8},{8,5},{9,12},{12,9},{13,14},{14,13},{15,10... | collective-permute-start | bytes 294920 | tf_op jit(solution)/shard_map/ppermute | solution.py:125
  2.4 1.9 %shard_map.37 = (bf16[768,896]{1,0:T(8,128)(2,1)S(1)}, bf16[64,1768]{1,0:T(8,128)(2,1)S(1)}) custom-call(bf16[896,768]{1,0:T(8,128)(2,1)} %q_hbm.1, bf16[64,768]{1,0:T(8,128)(2,1)} %k_hbm.1, bf16[64,1000]{1,0:T(8,128)(2,1)} %l_hbm.1), custom_call_target="tpu_custom_call" | custom-call | tf_op jit(solution)/shard_map/pallas_call | solution.py:48
  4.4 0.8 %collective-permute-start.7 = (bf16[64,1768]{1,0:T(8,128)(2,1)S(1)}, bf16[64,1768]{1,0:T(8,128)(2,1)S(1)}, u32[]{:S(2)}, u32[]{:S(2)}) collective-permute-start(bf16[64,1768]{1,0:T(8,128)(2,1)S(1)} %get-tuple-element.28.refs_1_), channel_id=1, source_target_pairs={{0,1},{1,0},{4,5},{5,4},{8,9},{9,8},{12,13},{13,12},{14,15},{15,14... | collective-permute-start | bytes 678920 | tf_op jit(solution)/shard_map/ppermute | solution.py:125
  5.2 1.7 %collective-permute-start.6 = (bf16[64,1768]{1,0:T(8,128)(2,1)S(1)}, bf16[64,1768]{1,0:T(8,128)(2,1)S(1)}, u32[]{:S(2)}, u32[]{:S(2)}) collective-permute-start(bf16[64,1768]{1,0:T(8,128)(2,1)S(1)} %get-tuple-element.28.refs_1_), channel_id=1, source_target_pairs={{0,5},{1,2},{4,9},{5,0},{8,13},{9,4},{12,15},{13,8},{14,11},{15,12... | collective-permute-start | bytes 678920 | tf_op jit(solution)/shard_map/ppermute | solution.py:125
  6.9 0.1 collective-permute-done.1
  7.0 2.0 %collective-permute-start.2 = (bf16[64,1768]{1,0:T(8,128)(2,1)S(1)}, bf16[64,1768]{1,0:T(8,128)(2,1)S(1)}, u32[]{:S(2)}, u32[]{:S(2)}) collective-permute-start(bf16[64,1768]{1,0:T(8,128)(2,1)S(1)} %constant_dynamic-update-slice_fusion.refs_3_), channel_id=1, source_target_pairs={{0,5},{1,2},{4,9},{5,0},{8,13},{9,4},{12,15},{13,8},{14,11},{15,12... | collective-permute-start | bytes 678920 | tf_op jit(solution)/shard_map/ppermute | solution.py:125
  9.0 1.1 %shard_map.38 = (f32[1,896]{1,0:T(1,128)S(1)}, f32[1,896]{1,0:T(1,128)S(1)}, f32[1000,896]{1,0:T(8,128)S(1)}) custom-call(bf16[768,896]{1,0:T(8,128)(2,1)S(1)} %get-tuple-element.27.refs_0_, bf16[64,1768]{1,0:T(8,128)(2,1)S(1)} %get-tuple-element.28.refs_1_, bf16[64,1768]{1,0:T(8,128)(2,1)S(1)} %collective-permute-done.7.refs_2_, ...), custom_call_target="tpu_custom_call" | custom-call | tf_op jit(solution)/shard_map/pallas_call | solution.py:109
  10.1 0.5 %collective-permute-done.6.refs_2_ = bf16[64,1768]{1,0:T(8,128)(2,1)S(1)} collective-permute-done((bf16[64,1768]{1,0:T(8,128)(2,1)S(1)}, bf16[64,1768]{1,0:T(8,128)(2,1)S(1)}, u32[]{:S(2)}, u32[]{:S(2)}) %collective-permute-start.6) | collective-permute-done | bytes 226336 | tf_op jit(solution)/shard_map/ppermute | solution.py:125
  10.6 1.9 %collective-permute-start.8 = (bf16[64,1768]{1,0:T(8,128)(2,1)S(1)}, bf16[64,1768]{1,0:T(8,128)(2,1)S(1)}, u32[]{:S(2)}, u32[]{:S(2)}) collective-permute-start(bf16[64,1768]{1,0:T(8,128)(2,1)S(1)} %collective-permute-done.6.refs_2_), channel_id=1, source_target_pairs={{0,3},{1,4},{4,1},{5,8},{8,5},{9,12},{12,9},{13,14},{14,13},{15,10... | collective-permute-start | bytes 678920 | tf_op jit(solution)/shard_map/ppermute | solution.py:125
  12.6 0.5 %collective-permute-done.2.refs_4_ = bf16[64,1768]{1,0:T(8,128)(2,1)S(1)} collective-permute-done((bf16[64,1768]{1,0:T(8,128)(2,1)S(1)}, bf16[64,1768]{1,0:T(8,128)(2,1)S(1)}, u32[]{:S(2)}, u32[]{:S(2)}) %collective-permute-start.2) | collective-permute-done | bytes 226336 | tf_op jit(solution)/shard_map/ppermute | solution.py:125
  13.1 1.7 %collective-permute-start.3 = (bf16[64,1768]{1,0:T(8,128)(2,1)S(1)}, bf16[64,1768]{1,0:T(8,128)(2,1)S(1)}, u32[]{:S(2)}, u32[]{:S(2)}) collective-permute-start(bf16[64,1768]{1,0:T(8,128)(2,1)S(1)} %collective-permute-done.2.refs_4_), channel_id=1, source_target_pairs={{0,3},{1,4},{4,1},{5,8},{8,5},{9,12},{12,9},{13,14},{14,13},{15,10... | collective-permute-start | bytes 678920 | tf_op jit(solution)/shard_map/ppermute | solution.py:125
  14.7 0.1 collective-permute-start.11
  14.9 1.4 %collective-permute-done.8.refs_2_ = bf16[64,1768]{1,0:T(8,128)(2,1)S(1)} collective-permute-done((bf16[64,1768]{1,0:T(8,128)(2,1)S(1)}, bf16[64,1768]{1,0:T(8,128)(2,1)S(1)}, u32[]{:S(2)}, u32[]{:S(2)}) %collective-permute-start.8) | collective-permute-done | bytes 226336 | tf_op jit(solution)/shard_map/ppermute | solution.py:125
  16.3 2.1 %collective-permute-start.14 = (bf16[64,1768]{1,0:T(8,128)(2,1)S(1)}, bf16[64,1768]{1,0:T(8,128)(2,1)S(1)}, u32[]{:S(2)}, u32[]{:S(2)}) collective-permute-start(bf16[64,1768]{1,0:T(8,128)(2,1)S(1)} %collective-permute-done.8.refs_2_), channel_id=1, source_target_pairs={{0,5},{1,2},{4,9},{5,0},{8,13},{9,4},{12,15},{13,8},{14,11},{15,12... | collective-permute-start | bytes 678920 | tf_op jit(solution)/shard_map/ppermute | solution.py:125
  18.4 0.5 %collective-permute-start.9 = (bf16[64,1768]{1,0:T(8,128)(2,1)S(1)}, bf16[64,1768]{1,0:T(8,128)(2,1)S(1)}, u32[]{:S(2)}, u32[]{:S(2)}) collective-permute-start(bf16[64,1768]{1,0:T(8,128)(2,1)S(1)} %collective-permute-done.8.refs_2_), channel_id=1, source_target_pairs={{0,1},{1,0},{4,5},{5,4},{8,9},{9,8},{12,13},{13,12},{14,15},{15,14... | collective-permute-start | bytes 678920 | tf_op jit(solution)/shard_map/ppermute | solution.py:125
  18.9 1.7 %collective-permute-start.4 = (bf16[64,1768]{1,0:T(8,128)(2,1)S(1)}, bf16[64,1768]{1,0:T(8,128)(2,1)S(1)}, u32[]{:S(2)}, u32[]{:S(2)}) collective-permute-start(bf16[64,1768]{1,0:T(8,128)(2,1)S(1)} %collective-permute-done.3.refs_4_), channel_id=1, source_target_pairs={{0,5},{1,2},{4,9},{5,0},{8,13},{9,4},{12,15},{13,8},{14,11},{15,12... | collective-permute-start | bytes 678920 | tf_op jit(solution)/shard_map/ppermute | solution.py:125
  20.5 1.3 %shard_map.39 = (f32[1,896]{1,0:T(1,128)S(1)}, f32[1,896]{1,0:T(1,128)S(1)}, f32[1000,896]{1,0:T(8,128)S(1)}) custom-call(bf16[768,896]{1,0:T(8,128)(2,1)S(1)} %get-tuple-element.27.refs_0_, bf16[64,1768]{1,0:T(8,128)(2,1)S(1)} %collective-permute-done.10.refs_1_, bf16[64,1768]{1,0:T(8,128)(2,1)S(1)} %collective-permute-done.6.refs_2_, ...), custom_call_target="tpu_custom_call" | custom-call | tf_op jit(solution)/shard_map/pallas_call | solution.py:109
  21.9 0.2 collective-permute-done.14.refs_2_
  22.1 0.4 %collective-permute-start.15 = (bf16[64,1768]{1,0:T(8,128)(2,1)S(1)}, bf16[64,1768]{1,0:T(8,128)(2,1)S(1)}, u32[]{:S(2)}, u32[]{:S(2)}) collective-permute-start(bf16[64,1768]{1,0:T(8,128)(2,1)S(1)} %collective-permute-done.14.refs_2_), channel_id=1, source_target_pairs={{0,1},{1,0},{4,5},{5,4},{8,9},{9,8},{12,13},{13,12},{14,15},{15,14... | collective-permute-start | bytes 678920 | tf_op jit(solution)/shard_map/ppermute | solution.py:125
  22.5 1.5 %shard_map.40 = (f32[1,896]{1,0:T(1,128)S(1)}, f32[1,896]{1,0:T(1,128)S(1)}, f32[1000,896]{1,0:T(8,128)S(1)}) custom-call(bf16[768,896]{1,0:T(8,128)(2,1)S(1)} %get-tuple-element.27.refs_0_, bf16[64,1768]{1,0:T(8,128)(2,1)S(1)} %collective-permute-done.5.refs_1_, bf16[64,1768]{1,0:T(8,128)(2,1)S(1)} %collective-permute-done.8.refs_2_, ...), custom_call_target="tpu_custom_call" | custom-call | tf_op jit(solution)/shard_map/pallas_call | solution.py:109
  24.0 0.5 %collective-permute-done.4.refs_1_ = bf16[64,1768]{1,0:T(8,128)(2,1)S(1)} collective-permute-done((bf16[64,1768]{1,0:T(8,128)(2,1)S(1)}, bf16[64,1768]{1,0:T(8,128)(2,1)S(1)}, u32[]{:S(2)}, u32[]{:S(2)}) %collective-permute-start.4) | collective-permute-done | bytes 226336 | tf_op jit(solution)/shard_map/ppermute | solution.py:125
  24.5 0.1 collective-permute-start.12
  24.6 1.5 %shard_map.41 = (f32[1,896]{1,0:T(1,128)S(1)}, f32[1,896]{1,0:T(1,128)S(1)}, f32[1000,896]{1,0:T(8,128)S(1)}) custom-call(bf16[768,896]{1,0:T(8,128)(2,1)S(1)} %get-tuple-element.27.refs_0_, bf16[64,1768]{1,0:T(8,128)(2,1)S(1)} %collective-permute-done.13.refs_1_, bf16[64,1768]{1,0:T(8,128)(2,1)S(1)} %collective-permute-done.14.refs_2_, ...), custom_call_target="tpu_custom_call" | custom-call | tf_op jit(solution)/shard_map/pallas_call | solution.py:109
  26.2 2.1 %shard_map.42 = bf16[1000,896]{1,0:T(8,128)(2,1)} custom-call(bf16[768,896]{1,0:T(8,128)(2,1)S(1)} %get-tuple-element.27.refs_0_, bf16[64,1768]{1,0:T(8,128)(2,1)S(1)} %collective-permute-done.4.refs_1_, bf16[64,1768]{1,0:T(8,128)(2,1)S(1)} %collective-permute-done.12.refs_2_, f32[1,896]{1,0:T(1,128)S(1)} %get-tuple-element.46.refs_3_, ...), custom_call_target="tpu_custom_call" | custom-call | tf_op jit(solution)/shard_map/pallas_call | solution.py:109
  (16 shorter events, 0.2 us)
Async XLA Ops:
  0.0 6.9 %collective-permute-start = (bf16[64,768]{1,0:T(8,128)(2,1)}, bf16[64,768]{1,0:T(8,128)(2,1)S(1)}, u32[]{:S(2)}, u32[]{:S(2)}) collective-permute-start(bf16[64,768]{1,0:T(8,128)(2,1)} %k_hbm.1), channel_id=1, source_target_pairs={{0,3},{1,4},{4,1},{5,8},{8,5},{9,12},{12,9},{13,14},{14,13},{15,10... | collective-permute-start | bytes 294920 | tf_op jit(solution)/shard_map/ppermute | solution.py:125
  2.4 4.6 %collective-permute-start.1 = (bf16[64,1000]{1,0:T(8,128)(2,1)}, bf16[64,1000]{1,0:T(8,128)(2,1)S(1)}, u32[]{:S(2)}, u32[]{:S(2)}) collective-permute-start(bf16[64,1000]{1,0:T(8,128)(2,1)} %l_hbm.1), channel_id=1, source_target_pairs={{0,3},{1,4},{4,1},{5,8},{8,5},{9,12},{12,9},{13,14},{14,13},{15,10... | collective-permute-start | bytes 384008 | tf_op jit(solution)/shard_map/ppermute | solution.py:125
  4.4 4.6 %collective-permute-start.7 = (bf16[64,1768]{1,0:T(8,128)(2,1)S(1)}, bf16[64,1768]{1,0:T(8,128)(2,1)S(1)}, u32[]{:S(2)}, u32[]{:S(2)}) collective-permute-start(bf16[64,1768]{1,0:T(8,128)(2,1)S(1)} %get-tuple-element.28.refs_1_), channel_id=1, source_target_pairs={{0,1},{1,0},{4,5},{5,4},{8,9},{9,8},{12,13},{13,12},{14,15},{15,14... | collective-permute-start | bytes 678920 | tf_op jit(solution)/shard_map/ppermute | solution.py:125
  5.2 5.4 %collective-permute-start.6 = (bf16[64,1768]{1,0:T(8,128)(2,1)S(1)}, bf16[64,1768]{1,0:T(8,128)(2,1)S(1)}, u32[]{:S(2)}, u32[]{:S(2)}) collective-permute-start(bf16[64,1768]{1,0:T(8,128)(2,1)S(1)} %get-tuple-element.28.refs_1_), channel_id=1, source_target_pairs={{0,5},{1,2},{4,9},{5,0},{8,13},{9,4},{12,15},{13,8},{14,11},{15,12... | collective-permute-start | bytes 678920 | tf_op jit(solution)/shard_map/ppermute | solution.py:125
  7.0 6.0 %collective-permute-start.2 = (bf16[64,1768]{1,0:T(8,128)(2,1)S(1)}, bf16[64,1768]{1,0:T(8,128)(2,1)S(1)}, u32[]{:S(2)}, u32[]{:S(2)}) collective-permute-start(bf16[64,1768]{1,0:T(8,128)(2,1)S(1)} %constant_dynamic-update-slice_fusion.refs_3_), channel_id=1, source_target_pairs={{0,5},{1,2},{4,9},{5,0},{8,13},{9,4},{12,15},{13,8},{14,11},{15,12... | collective-permute-start | bytes 678920 | tf_op jit(solution)/shard_map/ppermute | solution.py:125
  10.6 5.7 %collective-permute-start.8 = (bf16[64,1768]{1,0:T(8,128)(2,1)S(1)}, bf16[64,1768]{1,0:T(8,128)(2,1)S(1)}, u32[]{:S(2)}, u32[]{:S(2)}) collective-permute-start(bf16[64,1768]{1,0:T(8,128)(2,1)S(1)} %collective-permute-done.6.refs_2_), channel_id=1, source_target_pairs={{0,3},{1,4},{4,1},{5,8},{8,5},{9,12},{12,9},{13,14},{14,13},{15,10... | collective-permute-start | bytes 678920 | tf_op jit(solution)/shard_map/ppermute | solution.py:125
  12.6 5.8 %collective-permute-start.10 = (bf16[64,1768]{1,0:T(8,128)(2,1)S(1)}, bf16[64,1768]{1,0:T(8,128)(2,1)S(1)}, u32[]{:S(2)}, u32[]{:S(2)}) collective-permute-start(bf16[64,1768]{1,0:T(8,128)(2,1)S(1)} %constant_dynamic-update-slice_fusion.refs_3_), channel_id=1, source_target_pairs={{0,1},{1,0},{4,5},{5,4},{8,9},{9,8},{12,13},{13,12},{14,15},{15,14... | collective-permute-start | bytes 678920 | tf_op jit(solution)/shard_map/ppermute | solution.py:125
  13.1 5.8 %collective-permute-start.3 = (bf16[64,1768]{1,0:T(8,128)(2,1)S(1)}, bf16[64,1768]{1,0:T(8,128)(2,1)S(1)}, u32[]{:S(2)}, u32[]{:S(2)}) collective-permute-start(bf16[64,1768]{1,0:T(8,128)(2,1)S(1)} %collective-permute-done.2.refs_4_), channel_id=1, source_target_pairs={{0,3},{1,4},{4,1},{5,8},{8,5},{9,12},{12,9},{13,14},{14,13},{15,10... | collective-permute-start | bytes 678920 | tf_op jit(solution)/shard_map/ppermute | solution.py:125
  14.7 5.8 %collective-permute-start.11 = (bf16[64,1768]{1,0:T(8,128)(2,1)S(1)}, bf16[64,1768]{1,0:T(8,128)(2,1)S(1)}, u32[]{:S(2)}, u32[]{:S(2)}) collective-permute-start(bf16[64,1768]{1,0:T(8,128)(2,1)S(1)} %collective-permute-done.6.refs_2_), channel_id=1, source_target_pairs={{0,1},{1,0},{4,5},{5,4},{8,9},{9,8},{12,13},{13,12},{14,15},{15,14... | collective-permute-start | bytes 678920 | tf_op jit(solution)/shard_map/ppermute | solution.py:125
  16.3 5.8 %collective-permute-start.14 = (bf16[64,1768]{1,0:T(8,128)(2,1)S(1)}, bf16[64,1768]{1,0:T(8,128)(2,1)S(1)}, u32[]{:S(2)}, u32[]{:S(2)}) collective-permute-start(bf16[64,1768]{1,0:T(8,128)(2,1)S(1)} %collective-permute-done.8.refs_2_), channel_id=1, source_target_pairs={{0,5},{1,2},{4,9},{5,0},{8,13},{9,4},{12,15},{13,8},{14,11},{15,12... | collective-permute-start | bytes 678920 | tf_op jit(solution)/shard_map/ppermute | solution.py:125
  18.4 4.1 %collective-permute-start.5 = (bf16[64,1768]{1,0:T(8,128)(2,1)S(1)}, bf16[64,1768]{1,0:T(8,128)(2,1)S(1)}, u32[]{:S(2)}, u32[]{:S(2)}) collective-permute-start(bf16[64,1768]{1,0:T(8,128)(2,1)S(1)} %collective-permute-done.2.refs_4_), channel_id=1, source_target_pairs={{0,1},{1,0},{4,5},{5,4},{8,9},{9,8},{12,13},{13,12},{14,15},{15,14... | collective-permute-start | bytes 678920 | tf_op jit(solution)/shard_map/ppermute | solution.py:125
  18.4 4.1 %collective-permute-start.9 = (bf16[64,1768]{1,0:T(8,128)(2,1)S(1)}, bf16[64,1768]{1,0:T(8,128)(2,1)S(1)}, u32[]{:S(2)}, u32[]{:S(2)}) collective-permute-start(bf16[64,1768]{1,0:T(8,128)(2,1)S(1)} %collective-permute-done.8.refs_2_), channel_id=1, source_target_pairs={{0,1},{1,0},{4,5},{5,4},{8,9},{9,8},{12,13},{13,12},{14,15},{15,14... | collective-permute-start | bytes 678920 | tf_op jit(solution)/shard_map/ppermute | solution.py:125
  18.9 5.6 %collective-permute-start.4 = (bf16[64,1768]{1,0:T(8,128)(2,1)S(1)}, bf16[64,1768]{1,0:T(8,128)(2,1)S(1)}, u32[]{:S(2)}, u32[]{:S(2)}) collective-permute-start(bf16[64,1768]{1,0:T(8,128)(2,1)S(1)} %collective-permute-done.3.refs_4_), channel_id=1, source_target_pairs={{0,5},{1,2},{4,9},{5,0},{8,13},{9,4},{12,15},{13,8},{14,11},{15,12... | collective-permute-start | bytes 678920 | tf_op jit(solution)/shard_map/ppermute | solution.py:125
  21.8 2.8 %collective-permute-start.13 = (bf16[64,1768]{1,0:T(8,128)(2,1)S(1)}, bf16[64,1768]{1,0:T(8,128)(2,1)S(1)}, u32[]{:S(2)}, u32[]{:S(2)}) collective-permute-start(bf16[64,1768]{1,0:T(8,128)(2,1)S(1)} %collective-permute-done.3.refs_4_), channel_id=1, source_target_pairs={{0,1},{1,0},{4,5},{5,4},{8,9},{9,8},{12,13},{13,12},{14,15},{15,14... | collective-permute-start | bytes 678920 | tf_op jit(solution)/shard_map/ppermute | solution.py:125
  22.1 2.6 %collective-permute-start.15 = (bf16[64,1768]{1,0:T(8,128)(2,1)S(1)}, bf16[64,1768]{1,0:T(8,128)(2,1)S(1)}, u32[]{:S(2)}, u32[]{:S(2)}) collective-permute-start(bf16[64,1768]{1,0:T(8,128)(2,1)S(1)} %collective-permute-done.14.refs_2_), channel_id=1, source_target_pairs={{0,1},{1,0},{4,5},{5,4},{8,9},{9,8},{12,13},{13,12},{14,15},{15,14... | collective-permute-start | bytes 678920 | tf_op jit(solution)/shard_map/ppermute | solution.py:125
  24.5 1.6 %collective-permute-start.12 = (bf16[64,1768]{1,0:T(8,128)(2,1)S(1)}, bf16[64,1768]{1,0:T(8,128)(2,1)S(1)}, u32[]{:S(2)}, u32[]{:S(2)}) collective-permute-start(bf16[64,1768]{1,0:T(8,128)(2,1)S(1)} %collective-permute-done.4.refs_1_), channel_id=1, source_target_pairs={{0,1},{1,0},{4,5},{5,4},{8,9},{9,8},{12,13},{13,12},{14,15},{15,14... | collective-permute-start | bytes 678920 | tf_op jit(solution)/shard_map/ppermute | solution.py:125

commit v4 on v3

--- a/solution.py
+++ b/solution.py
@@ -28,18 +28,20 @@
 
 
 def begin(q_hbm, k_hbm, l_hbm, q_ref, own_ref, q_in, k_in, l_in, sem):
-    copies = [
-        pltpu.make_async_copy(source, target, sem.at[n])
-        for n, (source, target) in enumerate([(k_hbm, k_in), (l_hbm, l_in), (q_hbm, q_in)])
-    ]
+    rows, width = q_in.shape
+    middle = rows // 256 * 128
+    spans = [(0, middle), (middle, rows)]
+    parts = [(k_hbm, k_in), (l_hbm, l_in)] + [(q_hbm.at[low:high], q_in.at[low:high]) for low, high in spans]
+    copies = [pltpu.make_async_copy(source, target, sem.at[n]) for n, (source, target) in enumerate(parts)]
     for copy in copies:
         copy.start()
-    for copy in copies:
+    copies[0].wait()
+    own_ref[:, :width] = k_in[...]
+    copies[1].wait()
+    own_ref[:, width:] = l_in[...]
+    for copy, (low, high) in zip(copies[2:], spans):
         copy.wait()
-    width = k_in.shape[1]
-    own_ref[:, :width] = k_in[...]
-    own_ref[:, width:] = l_in[...]
-    q_ref[...] = q_in[...].T
+        q_ref[:, low:high] = q_in[low:high, :].T
 
 
 def begin_call(queries, key_rows, label_rows):
@@ -57,7 +59,7 @@
             pltpu.VMEM((rows, width), BF16),
             pltpu.VMEM((count, width), BF16),
             pltpu.VMEM((count, classes), BF16),
-            pltpu.SemaphoreType.DMA((3,)),
+            pltpu.SemaphoreType.DMA((4,)),
         ],
         compiler_params=PARAMS,
     )(*operands)

time: 28.4 us -> 28.2 us (level)
  transfers between devices with their start and end apart: 16 -> 16, of which waited for: 6 -> 6; matrix products, arithmetic and copies ran while one was open for 0% -> 0% of each run, Pallas kernels for 26% -> 25%
where the time goes in v4:
time: 28.2 us; the launch traced here: 28.1 us
  starting transfers between devices  15.5 us (55%)
  Pallas kernels  9.21 us (33%)
  waiting for transfers between devices  3.26 us (12%)
    ppermute x16, starting transfers between devices, send(): return lax.ppermute(x, AXES, pairs)  15.5 us
    pallas_call x5, Pallas kernels, absorb_call(): pl.pallas_call(functools.partial(absorb, width, len(pieces), not state, l...  7.48 us
    ppermute x16, waiting for transfers between devices, send(): return lax.ppermute(x, AXES, pairs)  3.26 us
    pallas_call x1, Pallas kernels, begin_call(): pl.pallas_call(begin, out_shape=[jax.ShapeDtypeStruct((width, rows), BF16...  1.72 us
  transfers between devices with their start and end apart: 16, of which 6 were waited for; matrix products, arithmetic and copies ran while one was open for 0% of the time, Pallas kernels for 25%

profile of v4, /device:TPU:0, one launch (start us, length us, event | category | flops | bytes accessed | tf_op | source)
XLA Modules:
  0.0 28.1 jit_solution(5222018984023035246)
XLA Ops:
  0.0 2.4 %collective-permute-start = (bf16[64,768]{1,0:T(8,128)(2,1)}, bf16[64,768]{1,0:T(8,128)(2,1)S(1)}, u32[]{:S(2)}, u32[]{:S(2)}) collective-permute-start(bf16[64,768]{1,0:T(8,128)(2,1)} %k_hbm.1), channel_id=1, source_target_pairs={{0,3},{1,4},{4,1},{5,8},{8,5},{9,12},{12,9},{13,14},{14,13},{15,10... | collective-permute-start | bytes 294920 | tf_op jit(solution)/shard_map/ppermute | solution.py:127
  2.4 1.7 %shard_map.37 = (bf16[768,896]{1,0:T(8,128)(2,1)S(1)}, bf16[64,1768]{1,0:T(8,128)(2,1)S(1)}) custom-call(bf16[896,768]{1,0:T(8,128)(2,1)} %q_hbm.1, bf16[64,768]{1,0:T(8,128)(2,1)} %k_hbm.1, bf16[64,1000]{1,0:T(8,128)(2,1)} %l_hbm.1), custom_call_target="tpu_custom_call" | custom-call | tf_op jit(solution)/shard_map/pallas_call | solution.py:50
  4.2 0.8 %collective-permute-start.7 = (bf16[64,1768]{1,0:T(8,128)(2,1)S(1)}, bf16[64,1768]{1,0:T(8,128)(2,1)S(1)}, u32[]{:S(2)}, u32[]{:S(2)}) collective-permute-start(bf16[64,1768]{1,0:T(8,128)(2,1)S(1)} %get-tuple-element.28.refs_1_), channel_id=1, source_target_pairs={{0,1},{1,0},{4,5},{5,4},{8,9},{9,8},{12,13},{13,12},{14,15},{15,14... | collective-permute-start | bytes 678920 | tf_op jit(solution)/shard_map/ppermute | solution.py:127
  5.0 1.7 %collective-permute-start.6 = (bf16[64,1768]{1,0:T(8,128)(2,1)S(1)}, bf16[64,1768]{1,0:T(8,128)(2,1)S(1)}, u32[]{:S(2)}, u32[]{:S(2)}) collective-permute-start(bf16[64,1768]{1,0:T(8,128)(2,1)S(1)} %get-tuple-element.28.refs_1_), channel_id=1, source_target_pairs={{0,5},{1,2},{4,9},{5,0},{8,13},{9,4},{12,15},{13,8},{14,11},{15,12... | collective-permute-start | bytes 678920 | tf_op jit(solution)/shard_map/ppermute | solution.py:127
  6.7 0.3 %collective-permute-done.1 = bf16[64,1000]{1,0:T(8,128)(2,1)S(1)} collective-permute-done((bf16[64,1000]{1,0:T(8,128)(2,1)}, bf16[64,1000]{1,0:T(8,128)(2,1)S(1)}, u32[]{:S(2)}, u32[]{:S(2)}) %collective-permute-start.1) | collective-permute-done | bytes 128032 | tf_op jit(solution)/shard_map/ppermute | solution.py:127
  7.0 2.0 %collective-permute-start.2 = (bf16[64,1768]{1,0:T(8,128)(2,1)S(1)}, bf16[64,1768]{1,0:T(8,128)(2,1)S(1)}, u32[]{:S(2)}, u32[]{:S(2)}) collective-permute-start(bf16[64,1768]{1,0:T(8,128)(2,1)S(1)} %constant_dynamic-update-slice_fusion.refs_3_), channel_id=1, source_target_pairs={{0,5},{1,2},{4,9},{5,0},{8,13},{9,4},{12,15},{13,8},{14,11},{15,12... | collective-permute-start | bytes 678920 | tf_op jit(solution)/shard_map/ppermute | solution.py:127
  9.0 1.1 %shard_map.38 = (f32[1,896]{1,0:T(1,128)S(1)}, f32[1,896]{1,0:T(1,128)S(1)}, f32[1000,896]{1,0:T(8,128)S(1)}) custom-call(bf16[768,896]{1,0:T(8,128)(2,1)S(1)} %get-tuple-element.27.refs_0_, bf16[64,1768]{1,0:T(8,128)(2,1)S(1)} %get-tuple-element.28.refs_1_, bf16[64,1768]{1,0:T(8,128)(2,1)S(1)} %collective-permute-done.7.refs_2_, ...), custom_call_target="tpu_custom_call" | custom-call | tf_op jit(solution)/shard_map/pallas_call | solution.py:111
  10.1 0.3 %collective-permute-done.6.refs_2_ = bf16[64,1768]{1,0:T(8,128)(2,1)S(1)} collective-permute-done((bf16[64,1768]{1,0:T(8,128)(2,1)S(1)}, bf16[64,1768]{1,0:T(8,128)(2,1)S(1)}, u32[]{:S(2)}, u32[]{:S(2)}) %collective-permute-start.6) | collective-permute-done | bytes 226336 | tf_op jit(solution)/shard_map/ppermute | solution.py:127
  10.4 1.9 %collective-permute-start.8 = (bf16[64,1768]{1,0:T(8,128)(2,1)S(1)}, bf16[64,1768]{1,0:T(8,128)(2,1)S(1)}, u32[]{:S(2)}, u32[]{:S(2)}) collective-permute-start(bf16[64,1768]{1,0:T(8,128)(2,1)S(1)} %collective-permute-done.6.refs_2_), channel_id=1, source_target_pairs={{0,3},{1,4},{4,1},{5,8},{8,5},{9,12},{12,9},{13,14},{14,13},{15,10... | collective-permute-start | bytes 678920 | tf_op jit(solution)/shard_map/ppermute | solution.py:127
  12.4 0.5 %collective-permute-done.2.refs_4_ = bf16[64,1768]{1,0:T(8,128)(2,1)S(1)} collective-permute-done((bf16[64,1768]{1,0:T(8,128)(2,1)S(1)}, bf16[64,1768]{1,0:T(8,128)(2,1)S(1)}, u32[]{:S(2)}, u32[]{:S(2)}) %collective-permute-start.2) | collective-permute-done | bytes 226336 | tf_op jit(solution)/shard_map/ppermute | solution.py:127
  12.9 1.7 %collective-permute-start.3 = (bf16[64,1768]{1,0:T(8,128)(2,1)S(1)}, bf16[64,1768]{1,0:T(8,128)(2,1)S(1)}, u32[]{:S(2)}, u32[]{:S(2)}) collective-permute-start(bf16[64,1768]{1,0:T(8,128)(2,1)S(1)} %collective-permute-done.2.refs_4_), channel_id=1, source_target_pairs={{0,3},{1,4},{4,1},{5,8},{8,5},{9,12},{12,9},{13,14},{14,13},{15,10... | collective-permute-start | bytes 678920 | tf_op jit(solution)/shard_map/ppermute | solution.py:127
  14.5 0.1 collective-permute-start.11
  14.7 1.4 %collective-permute-done.8.refs_2_ = bf16[64,1768]{1,0:T(8,128)(2,1)S(1)} collective-permute-done((bf16[64,1768]{1,0:T(8,128)(2,1)S(1)}, bf16[64,1768]{1,0:T(8,128)(2,1)S(1)}, u32[]{:S(2)}, u32[]{:S(2)}) %collective-permute-start.8) | collective-permute-done | bytes 226336 | tf_op jit(solution)/shard_map/ppermute | solution.py:127
  16.1 2.1 %collective-permute-start.14 = (bf16[64,1768]{1,0:T(8,128)(2,1)S(1)}, bf16[64,1768]{1,0:T(8,128)(2,1)S(1)}, u32[]{:S(2)}, u32[]{:S(2)}) collective-permute-start(bf16[64,1768]{1,0:T(8,128)(2,1)S(1)} %collective-permute-done.8.refs_2_), channel_id=1, source_target_pairs={{0,5},{1,2},{4,9},{5,0},{8,13},{9,4},{12,15},{13,8},{14,11},{15,12... | collective-permute-start | bytes 678920 | tf_op jit(solution)/shard_map/ppermute | solution.py:127
  18.2 0.5 %collective-permute-start.9 = (bf16[64,1768]{1,0:T(8,128)(2,1)S(1)}, bf16[64,1768]{1,0:T(8,128)(2,1)S(1)}, u32[]{:S(2)}, u32[]{:S(2)}) collective-permute-start(bf16[64,1768]{1,0:T(8,128)(2,1)S(1)} %collective-permute-done.8.refs_2_), channel_id=1, source_target_pairs={{0,1},{1,0},{4,5},{5,4},{8,9},{9,8},{12,13},{13,12},{14,15},{15,14... | collective-permute-start | bytes 678920 | tf_op jit(solution)/shard_map/ppermute | solution.py:127
  18.7 1.7 %collective-permute-start.4 = (bf16[64,1768]{1,0:T(8,128)(2,1)S(1)}, bf16[64,1768]{1,0:T(8,128)(2,1)S(1)}, u32[]{:S(2)}, u32[]{:S(2)}) collective-permute-start(bf16[64,1768]{1,0:T(8,128)(2,1)S(1)} %collective-permute-done.3.refs_4_), channel_id=1, source_target_pairs={{0,5},{1,2},{4,9},{5,0},{8,13},{9,4},{12,15},{13,8},{14,11},{15,12... | collective-permute-start | bytes 678920 | tf_op jit(solution)/shard_map/ppermute | solution.py:127
  20.3 1.3 %shard_map.39 = (f32[1,896]{1,0:T(1,128)S(1)}, f32[1,896]{1,0:T(1,128)S(1)}, f32[1000,896]{1,0:T(8,128)S(1)}) custom-call(bf16[768,896]{1,0:T(8,128)(2,1)S(1)} %get-tuple-element.27.refs_0_, bf16[64,1768]{1,0:T(8,128)(2,1)S(1)} %collective-permute-done.10.refs_1_, bf16[64,1768]{1,0:T(8,128)(2,1)S(1)} %collective-permute-done.6.refs_2_, ...), custom_call_target="tpu_custom_call" | custom-call | tf_op jit(solution)/shard_map/pallas_call | solution.py:111
  21.7 0.2 collective-permute-done.14.refs_2_
  21.9 0.4 %collective-permute-start.15 = (bf16[64,1768]{1,0:T(8,128)(2,1)S(1)}, bf16[64,1768]{1,0:T(8,128)(2,1)S(1)}, u32[]{:S(2)}, u32[]{:S(2)}) collective-permute-start(bf16[64,1768]{1,0:T(8,128)(2,1)S(1)} %collective-permute-done.14.refs_2_), channel_id=1, source_target_pairs={{0,1},{1,0},{4,5},{5,4},{8,9},{9,8},{12,13},{13,12},{14,15},{15,14... | collective-permute-start | bytes 678920 | tf_op jit(solution)/shard_map/ppermute | solution.py:127
  22.3 1.5 %shard_map.40 = (f32[1,896]{1,0:T(1,128)S(1)}, f32[1,896]{1,0:T(1,128)S(1)}, f32[1000,896]{1,0:T(8,128)S(1)}) custom-call(bf16[768,896]{1,0:T(8,128)(2,1)S(1)} %get-tuple-element.27.refs_0_, bf16[64,1768]{1,0:T(8,128)(2,1)S(1)} %collective-permute-done.5.refs_1_, bf16[64,1768]{1,0:T(8,128)(2,1)S(1)} %collective-permute-done.8.refs_2_, ...), custom_call_target="tpu_custom_call" | custom-call | tf_op jit(solution)/shard_map/pallas_call | solution.py:111
  23.8 0.5 %collective-permute-done.4.refs_1_ = bf16[64,1768]{1,0:T(8,128)(2,1)S(1)} collective-permute-done((bf16[64,1768]{1,0:T(8,128)(2,1)S(1)}, bf16[64,1768]{1,0:T(8,128)(2,1)S(1)}, u32[]{:S(2)}, u32[]{:S(2)}) %collective-permute-start.4) | collective-permute-done | bytes 226336 | tf_op jit(solution)/shard_map/ppermute | solution.py:127
  24.3 0.1 collective-permute-start.12
  24.4 1.5 %shard_map.41 = (f32[1,896]{1,0:T(1,128)S(1)}, f32[1,896]{1,0:T(1,128)S(1)}, f32[1000,896]{1,0:T(8,128)S(1)}) custom-call(bf16[768,896]{1,0:T(8,128)(2,1)S(1)} %get-tuple-element.27.refs_0_, bf16[64,1768]{1,0:T(8,128)(2,1)S(1)} %collective-permute-done.13.refs_1_, bf16[64,1768]{1,0:T(8,128)(2,1)S(1)} %collective-permute-done.14.refs_2_, ...), custom_call_target="tpu_custom_call" | custom-call | tf_op jit(solution)/shard_map/pallas_call | solution.py:111
  26.0 2.1 %shard_map.42 = bf16[1000,896]{1,0:T(8,128)(2,1)} custom-call(bf16[768,896]{1,0:T(8,128)(2,1)S(1)} %get-tuple-element.27.refs_0_, bf16[64,1768]{1,0:T(8,128)(2,1)S(1)} %collective-permute-done.4.refs_1_, bf16[64,1768]{1,0:T(8,128)(2,1)S(1)} %collective-permute-done.12.refs_2_, f32[1,896]{1,0:T(1,128)S(1)} %get-tuple-element.46.refs_3_, ...), custom_call_target="tpu_custom_call" | custom-call | tf_op jit(solution)/shard_map/pallas_call | solution.py:111
  (16 shorter events, 0.2 us)
Async XLA Ops:
  0.0 6.7 %collective-permute-start = (bf16[64,768]{1,0:T(8,128)(2,1)}, bf16[64,768]{1,0:T(8,128)(2,1)S(1)}, u32[]{:S(2)}, u32[]{:S(2)}) collective-permute-start(bf16[64,768]{1,0:T(8,128)(2,1)} %k_hbm.1), channel_id=1, source_target_pairs={{0,3},{1,4},{4,1},{5,8},{8,5},{9,12},{12,9},{13,14},{14,13},{15,10... | collective-permute-start | bytes 294920 | tf_op jit(solution)/shard_map/ppermute | solution.py:127
  2.4 4.6 %collective-permute-start.1 = (bf16[64,1000]{1,0:T(8,128)(2,1)}, bf16[64,1000]{1,0:T(8,128)(2,1)S(1)}, u32[]{:S(2)}, u32[]{:S(2)}) collective-permute-start(bf16[64,1000]{1,0:T(8,128)(2,1)} %l_hbm.1), channel_id=1, source_target_pairs={{0,3},{1,4},{4,1},{5,8},{8,5},{9,12},{12,9},{13,14},{14,13},{15,10... | collective-permute-start | bytes 384008 | tf_op jit(solution)/shard_map/ppermute | solution.py:127
  4.2 4.8 %collective-permute-start.7 = (bf16[64,1768]{1,0:T(8,128)(2,1)S(1)}, bf16[64,1768]{1,0:T(8,128)(2,1)S(1)}, u32[]{:S(2)}, u32[]{:S(2)}) collective-permute-start(bf16[64,1768]{1,0:T(8,128)(2,1)S(1)} %get-tuple-element.28.refs_1_), channel_id=1, source_target_pairs={{0,1},{1,0},{4,5},{5,4},{8,9},{9,8},{12,13},{13,12},{14,15},{15,14... | collective-permute-start | bytes 678920 | tf_op jit(solution)/shard_map/ppermute | solution.py:127
  5.0 5.4 %collective-permute-start.6 = (bf16[64,1768]{1,0:T(8,128)(2,1)S(1)}, bf16[64,1768]{1,0:T(8,128)(2,1)S(1)}, u32[]{:S(2)}, u32[]{:S(2)}) collective-permute-start(bf16[64,1768]{1,0:T(8,128)(2,1)S(1)} %get-tuple-element.28.refs_1_), channel_id=1, source_target_pairs={{0,5},{1,2},{4,9},{5,0},{8,13},{9,4},{12,15},{13,8},{14,11},{15,12... | collective-permute-start | bytes 678920 | tf_op jit(solution)/shard_map/ppermute | solution.py:127
  7.0 5.8 %collective-permute-start.2 = (bf16[64,1768]{1,0:T(8,128)(2,1)S(1)}, bf16[64,1768]{1,0:T(8,128)(2,1)S(1)}, u32[]{:S(2)}, u32[]{:S(2)}) collective-permute-start(bf16[64,1768]{1,0:T(8,128)(2,1)S(1)} %constant_dynamic-update-slice_fusion.refs_3_), channel_id=1, source_target_pairs={{0,5},{1,2},{4,9},{5,0},{8,13},{9,4},{12,15},{13,8},{14,11},{15,12... | collective-permute-start | bytes 678920 | tf_op jit(solution)/shard_map/ppermute | solution.py:127
  10.4 5.7 %collective-permute-start.8 = (bf16[64,1768]{1,0:T(8,128)(2,1)S(1)}, bf16[64,1768]{1,0:T(8,128)(2,1)S(1)}, u32[]{:S(2)}, u32[]{:S(2)}) collective-permute-start(bf16[64,1768]{1,0:T(8,128)(2,1)S(1)} %collective-permute-done.6.refs_2_), channel_id=1, source_target_pairs={{0,3},{1,4},{4,1},{5,8},{8,5},{9,12},{12,9},{13,14},{14,13},{15,10... | collective-permute-start | bytes 678920 | tf_op jit(solution)/shard_map/ppermute | solution.py:127
  12.4 5.8 %collective-permute-start.10 = (bf16[64,1768]{1,0:T(8,128)(2,1)S(1)}, bf16[64,1768]{1,0:T(8,128)(2,1)S(1)}, u32[]{:S(2)}, u32[]{:S(2)}) collective-permute-start(bf16[64,1768]{1,0:T(8,128)(2,1)S(1)} %constant_dynamic-update-slice_fusion.refs_3_), channel_id=1, source_target_pairs={{0,1},{1,0},{4,5},{5,4},{8,9},{9,8},{12,13},{13,12},{14,15},{15,14... | collective-permute-start | bytes 678920 | tf_op jit(solution)/shard_map/ppermute | solution.py:127
  12.9 5.8 %collective-permute-start.3 = (bf16[64,1768]{1,0:T(8,128)(2,1)S(1)}, bf16[64,1768]{1,0:T(8,128)(2,1)S(1)}, u32[]{:S(2)}, u32[]{:S(2)}) collective-permute-start(bf16[64,1768]{1,0:T(8,128)(2,1)S(1)} %collective-permute-done.2.refs_4_), channel_id=1, source_target_pairs={{0,3},{1,4},{4,1},{5,8},{8,5},{9,12},{12,9},{13,14},{14,13},{15,10... | collective-permute-start | bytes 678920 | tf_op jit(solution)/shard_map/ppermute | solution.py:127
  14.5 5.8 %collective-permute-start.11 = (bf16[64,1768]{1,0:T(8,128)(2,1)S(1)}, bf16[64,1768]{1,0:T(8,128)(2,1)S(1)}, u32[]{:S(2)}, u32[]{:S(2)}) collective-permute-start(bf16[64,1768]{1,0:T(8,128)(2,1)S(1)} %collective-permute-done.6.refs_2_), channel_id=1, source_target_pairs={{0,1},{1,0},{4,5},{5,4},{8,9},{9,8},{12,13},{13,12},{14,15},{15,14... | collective-permute-start | bytes 678920 | tf_op jit(solution)/shard_map/ppermute | solution.py:127
  16.1 5.8 %collective-permute-start.14 = (bf16[64,1768]{1,0:T(8,128)(2,1)S(1)}, bf16[64,1768]{1,0:T(8,128)(2,1)S(1)}, u32[]{:S(2)}, u32[]{:S(2)}) collective-permute-start(bf16[64,1768]{1,0:T(8,128)(2,1)S(1)} %collective-permute-done.8.refs_2_), channel_id=1, source_target_pairs={{0,5},{1,2},{4,9},{5,0},{8,13},{9,4},{12,15},{13,8},{14,11},{15,12... | collective-permute-start | bytes 678920 | tf_op jit(solution)/shard_map/ppermute | solution.py:127
  18.2 4.1 %collective-permute-start.5 = (bf16[64,1768]{1,0:T(8,128)(2,1)S(1)}, bf16[64,1768]{1,0:T(8,128)(2,1)S(1)}, u32[]{:S(2)}, u32[]{:S(2)}) collective-permute-start(bf16[64,1768]{1,0:T(8,128)(2,1)S(1)} %collective-permute-done.2.refs_4_), channel_id=1, source_target_pairs={{0,1},{1,0},{4,5},{5,4},{8,9},{9,8},{12,13},{13,12},{14,15},{15,14... | collective-permute-start | bytes 678920 | tf_op jit(solution)/shard_map/ppermute | solution.py:127
  18.2 4.1 %collective-permute-start.9 = (bf16[64,1768]{1,0:T(8,128)(2,1)S(1)}, bf16[64,1768]{1,0:T(8,128)(2,1)S(1)}, u32[]{:S(2)}, u32[]{:S(2)}) collective-permute-start(bf16[64,1768]{1,0:T(8,128)(2,1)S(1)} %collective-permute-done.8.refs_2_), channel_id=1, source_target_pairs={{0,1},{1,0},{4,5},{5,4},{8,9},{9,8},{12,13},{13,12},{14,15},{15,14... | collective-permute-start | bytes 678920 | tf_op jit(solution)/shard_map/ppermute | solution.py:127
  18.7 5.6 %collective-permute-start.4 = (bf16[64,1768]{1,0:T(8,128)(2,1)S(1)}, bf16[64,1768]{1,0:T(8,128)(2,1)S(1)}, u32[]{:S(2)}, u32[]{:S(2)}) collective-permute-start(bf16[64,1768]{1,0:T(8,128)(2,1)S(1)} %collective-permute-done.3.refs_4_), channel_id=1, source_target_pairs={{0,5},{1,2},{4,9},{5,0},{8,13},{9,4},{12,15},{13,8},{14,11},{15,12... | collective-permute-start | bytes 678920 | tf_op jit(solution)/shard_map/ppermute | solution.py:127
  21.6 2.8 %collective-permute-start.13 = (bf16[64,1768]{1,0:T(8,128)(2,1)S(1)}, bf16[64,1768]{1,0:T(8,128)(2,1)S(1)}, u32[]{:S(2)}, u32[]{:S(2)}) collective-permute-start(bf16[64,1768]{1,0:T(8,128)(2,1)S(1)} %collective-permute-done.3.refs_4_), channel_id=1, source_target_pairs={{0,1},{1,0},{4,5},{5,4},{8,9},{9,8},{12,13},{13,12},{14,15},{15,14... | collective-permute-start | bytes 678920 | tf_op jit(solution)/shard_map/ppermute | solution.py:127
  21.9 2.6 %collective-permute-start.15 = (bf16[64,1768]{1,0:T(8,128)(2,1)S(1)}, bf16[64,1768]{1,0:T(8,128)(2,1)S(1)}, u32[]{:S(2)}, u32[]{:S(2)}) collective-permute-start(bf16[64,1768]{1,0:T(8,128)(2,1)S(1)} %collective-permute-done.14.refs_2_), channel_id=1, source_target_pairs={{0,1},{1,0},{4,5},{5,4},{8,9},{9,8},{12,13},{13,12},{14,15},{15,14... | collective-permute-start | bytes 678920 | tf_op jit(solution)/shard_map/ppermute | solution.py:127
  24.3 1.6 %collective-permute-start.12 = (bf16[64,1768]{1,0:T(8,128)(2,1)S(1)}, bf16[64,1768]{1,0:T(8,128)(2,1)S(1)}, u32[]{:S(2)}, u32[]{:S(2)}) collective-permute-start(bf16[64,1768]{1,0:T(8,128)(2,1)S(1)} %collective-permute-done.4.refs_1_), channel_id=1, source_target_pairs={{0,1},{1,0},{4,5},{5,4},{8,9},{9,8},{12,13},{13,12},{14,15},{15,14... | collective-permute-start | bytes 678920 | tf_op jit(solution)/shard_map/ppermute | solution.py:127

commit v5 on v4

--- a/solution.py
+++ b/solution.py
@@ -149,9 +149,12 @@
             x_next = send(x, ways[step % 2])
             if step == 1:
                 y = absorb_before(1, y)
+            if step == half - 1:
+                y = absorb_before(half - 2, y)
             if step < half - 1:
                 y_next = send(y, ways[1 - step % 2])
-            groups[step] += [send(x, cores), y, send(y, cores)] + ([x] if step > 1 else [])
+            both = jnp.concatenate([x, y], axis=0)
+            groups[step] += [send(both, cores), y] + ([x] if step > 1 else [])
             x, y = x_next, y_next
         else:
             x = absorb_before(half - 1, x)

time: 28.2 us -> 28.2 us (level)
  starting transfers between devices: 15.5 us -> 15.2 us
    ppermute x16 -> x13, starting transfers between devices: 15.5 us -> 15.2 us  [send(): return lax.ppermute(x, AXES, pairs)]
    ppermute x16 -> x13, waiting for transfers between devices: 3.26 us -> 3.49 us  [send(): return lax.ppermute(x, AXES, pairs)]
  transfers between devices with their start and end apart: 16 -> 13, of which waited for: 6 -> 7; matrix products, arithmetic and copies ran while one was open for 0% -> 0% of each run, Pallas kernels for 25% -> 25%
where the time goes in v5:
time: 28.2 us; the launch traced here: 28.1 us
  starting transfers between devices  15.2 us (54%)
  Pallas kernels  9.2 us (33%)
  waiting for transfers between devices  3.49 us (12%)
    ppermute x13, starting transfers between devices, send(): return lax.ppermute(x, AXES, pairs)  15.2 us
    pallas_call x5, Pallas kernels, absorb_call(): pl.pallas_call(functools.partial(absorb, width, len(pieces), not state, l...  7.48 us
    ppermute x13, waiting for transfers between devices, send(): return lax.ppermute(x, AXES, pairs)  3.49 us
    pallas_call x1, Pallas kernels, begin_call(): pl.pallas_call(begin, out_shape=[jax.ShapeDtypeStruct((width, rows), BF16...  1.72 us
  transfers between devices with their start and end apart: 13, of which 7 were waited for; matrix products, arithmetic and copies ran while one was open for 0% of the time, Pallas kernels for 25%

profile of v5, /device:TPU:0, one launch (start us, length us, event | category | flops | bytes accessed | tf_op | source)
XLA Modules:
  0.0 28.1 jit_solution(3537665406924953672)
XLA Ops:
  0.0 2.4 %collective-permute-start = (bf16[64,768]{1,0:T(8,128)(2,1)}, bf16[64,768]{1,0:T(8,128)(2,1)S(1)}, u32[]{:S(2)}, u32[]{:S(2)}) collective-permute-start(bf16[64,768]{1,0:T(8,128)(2,1)} %k_hbm.1), channel_id=1, source_target_pairs={{0,3},{1,4},{4,1},{5,8},{8,5},{9,12},{12,9},{13,14},{14,13},{15,10... | collective-permute-start | bytes 294920 | tf_op jit(solution)/shard_map/ppermute | solution.py:127
  2.4 1.7 %shard_map.37 = (bf16[768,896]{1,0:T(8,128)(2,1)S(1)}, bf16[64,1768]{1,0:T(8,128)(2,1)S(1)}) custom-call(bf16[896,768]{1,0:T(8,128)(2,1)} %q_hbm.1, bf16[64,768]{1,0:T(8,128)(2,1)} %k_hbm.1, bf16[64,1000]{1,0:T(8,128)(2,1)} %l_hbm.1), custom_call_target="tpu_custom_call" | custom-call | tf_op jit(solution)/shard_map/pallas_call | solution.py:50
  4.2 0.8 %collective-permute-start.6 = (bf16[64,1768]{1,0:T(8,128)(2,1)S(1)}, bf16[64,1768]{1,0:T(8,128)(2,1)S(1)}, u32[]{:S(2)}, u32[]{:S(2)}) collective-permute-start(bf16[64,1768]{1,0:T(8,128)(2,1)S(1)} %get-tuple-element.32.refs_1_), channel_id=1, source_target_pairs={{0,1},{1,0},{4,5},{5,4},{8,9},{9,8},{12,13},{13,12},{14,15},{15,14... | collective-permute-start | bytes 678920 | tf_op jit(solution)/shard_map/ppermute | solution.py:127
  5.0 1.7 %collective-permute-start.5 = (bf16[64,1768]{1,0:T(8,128)(2,1)S(1)}, bf16[64,1768]{1,0:T(8,128)(2,1)S(1)}, u32[]{:S(2)}, u32[]{:S(2)}) collective-permute-start(bf16[64,1768]{1,0:T(8,128)(2,1)S(1)} %get-tuple-element.32.refs_1_), channel_id=1, source_target_pairs={{0,5},{1,2},{4,9},{5,0},{8,13},{9,4},{12,15},{13,8},{14,11},{15,12... | collective-permute-start | bytes 678920 | tf_op jit(solution)/shard_map/ppermute | solution.py:127
  6.7 0.3 %collective-permute-done.1 = bf16[64,1000]{1,0:T(8,128)(2,1)S(1)} collective-permute-done((bf16[64,1000]{1,0:T(8,128)(2,1)}, bf16[64,1000]{1,0:T(8,128)(2,1)S(1)}, u32[]{:S(2)}, u32[]{:S(2)}) %collective-permute-start.1) | collective-permute-done | bytes 128032 | tf_op jit(solution)/shard_map/ppermute | solution.py:127
  7.0 2.0 %collective-permute-start.2 = (bf16[64,1768]{1,0:T(8,128)(2,1)S(1)}, bf16[64,1768]{1,0:T(8,128)(2,1)S(1)}, u32[]{:S(2)}, u32[]{:S(2)}) collective-permute-start(bf16[64,1768]{1,0:T(8,128)(2,1)S(1)} %constant_dynamic-update-slice_fusion.refs_3_), channel_id=1, source_target_pairs={{0,5},{1,2},{4,9},{5,0},{8,13},{9,4},{12,15},{13,8},{14,11},{15,12... | collective-permute-start | bytes 678920 | tf_op jit(solution)/shard_map/ppermute | solution.py:127
  9.0 1.1 %shard_map.38 = (f32[1,896]{1,0:T(1,128)S(1)}, f32[1,896]{1,0:T(1,128)S(1)}, f32[1000,896]{1,0:T(8,128)S(1)}) custom-call(bf16[768,896]{1,0:T(8,128)(2,1)S(1)} %get-tuple-element.31.refs_0_, bf16[64,1768]{1,0:T(8,128)(2,1)S(1)} %get-tuple-element.32.refs_1_, bf16[64,1768]{1,0:T(8,128)(2,1)S(1)} %collective-permute-done.6.refs_2_, ...), custom_call_target="tpu_custom_call" | custom-call | tf_op jit(solution)/shard_map/pallas_call | solution.py:111
  10.1 0.3 %collective-permute-done.5.refs_2_ = bf16[64,1768]{1,0:T(8,128)(2,1)S(1)} collective-permute-done((bf16[64,1768]{1,0:T(8,128)(2,1)S(1)}, bf16[64,1768]{1,0:T(8,128)(2,1)S(1)}, u32[]{:S(2)}, u32[]{:S(2)}) %collective-permute-start.5) | collective-permute-done | bytes 226336 | tf_op jit(solution)/shard_map/ppermute | solution.py:127
  10.4 1.9 %collective-permute-start.7 = (bf16[64,1768]{1,0:T(8,128)(2,1)S(1)}, bf16[64,1768]{1,0:T(8,128)(2,1)S(1)}, u32[]{:S(2)}, u32[]{:S(2)}) collective-permute-start(bf16[64,1768]{1,0:T(8,128)(2,1)S(1)} %collective-permute-done.5.refs_2_), channel_id=1, source_target_pairs={{0,3},{1,4},{4,1},{5,8},{8,5},{9,12},{12,9},{13,14},{14,13},{15,10... | collective-permute-start | bytes 678920 | tf_op jit(solution)/shard_map/ppermute | solution.py:127
  12.4 0.1 collective-permute-start.10
  12.5 0.4 %collective-permute-done.2.refs_3_ = bf16[64,1768]{1,0:T(8,128)(2,1)S(1)} collective-permute-done((bf16[64,1768]{1,0:T(8,128)(2,1)S(1)}, bf16[64,1768]{1,0:T(8,128)(2,1)S(1)}, u32[]{:S(2)}, u32[]{:S(2)}) %collective-permute-start.2) | collective-permute-done | bytes 226336 | tf_op jit(solution)/shard_map/ppermute | solution.py:127
  12.9 1.7 %collective-permute-start.3 = (bf16[64,1768]{1,0:T(8,128)(2,1)S(1)}, bf16[64,1768]{1,0:T(8,128)(2,1)S(1)}, u32[]{:S(2)}, u32[]{:S(2)}) collective-permute-start(bf16[64,1768]{1,0:T(8,128)(2,1)S(1)} %collective-permute-done.2.refs_3_), channel_id=1, source_target_pairs={{0,3},{1,4},{4,1},{5,8},{8,5},{9,12},{12,9},{13,14},{14,13},{15,10... | collective-permute-start | bytes 678920 | tf_op jit(solution)/shard_map/ppermute | solution.py:127
  14.5 1.5 %collective-permute-done.7.refs_2_ = bf16[64,1768]{1,0:T(8,128)(2,1)S(1)} collective-permute-done((bf16[64,1768]{1,0:T(8,128)(2,1)S(1)}, bf16[64,1768]{1,0:T(8,128)(2,1)S(1)}, u32[]{:S(2)}, u32[]{:S(2)}) %collective-permute-start.7) | collective-permute-done | bytes 226336 | tf_op jit(solution)/shard_map/ppermute | solution.py:127
  16.1 2.1 %collective-permute-start.9 = (bf16[64,1768]{1,0:T(8,128)(2,1)S(1)}, bf16[64,1768]{1,0:T(8,128)(2,1)S(1)}, u32[]{:S(2)}, u32[]{:S(2)}) collective-permute-start(bf16[64,1768]{1,0:T(8,128)(2,1)S(1)} %collective-permute-done.7.refs_2_), channel_id=1, source_target_pairs={{0,5},{1,2},{4,9},{5,0},{8,13},{9,4},{12,15},{13,8},{14,11},{15,12... | collective-permute-start | bytes 678920 | tf_op jit(solution)/shard_map/ppermute | solution.py:127
  18.3 0.2 collective-permute-done.3.refs_3_
  18.5 1.8 %collective-permute-start.4 = (bf16[64,1768]{1,0:T(8,128)(2,1)S(1)}, bf16[64,1768]{1,0:T(8,128)(2,1)S(1)}, u32[]{:S(2)}, u32[]{:S(2)}) collective-permute-start(bf16[64,1768]{1,0:T(8,128)(2,1)S(1)} %collective-permute-done.3.refs_3_), channel_id=1, source_target_pairs={{0,5},{1,2},{4,9},{5,0},{8,13},{9,4},{12,15},{13,8},{14,11},{15,12... | collective-permute-start | bytes 678920 | tf_op jit(solution)/shard_map/ppermute | solution.py:127
  20.3 1.3 %shard_map.39 = (f32[1,896]{1,0:T(1,128)S(1)}, f32[1,896]{1,0:T(1,128)S(1)}, f32[1000,896]{1,0:T(8,128)S(1)}) custom-call(bf16[768,896]{1,0:T(8,128)(2,1)S(1)} %get-tuple-element.31.refs_0_, bf16[128,1768]{1,0:T(8,128)(2,1)S(1)} %collective-permute-done.10.refs_1_, bf16[64,1768]{1,0:T(8,128)(2,1)S(1)} %collective-permute-done.5.refs_2_, ...), custom_call_target="tpu_custom_call" | custom-call | tf_op jit(solution)/shard_map/pallas_call | solution.py:111
  21.6 0.2 collective-permute-done.9.refs_2_
  21.9 0.5 %collective-permute-start.12 = (bf16[128,1768]{1,0:T(8,128)(2,1)S(1)}, bf16[128,1768]{1,0:T(8,128)(2,1)S(1)}, u32[]{:S(2)}, u32[]{:S(2)}) collective-permute-start(bf16[128,1768]{1,0:T(8,128)(2,1)S(1)} %pad_maximum_fusion.2), channel_id=1, source_target_pairs={{0,1},{1,0},{4,5},{5,4},{8,9},{9,8},{12,13},{13,12},{14,15},{15,14... | collective-permute-start | bytes 1357832 | tf_op jit(solution)/shard_map/ppermute | solution.py:127
  22.4 1.5 %shard_map.40 = (f32[1,896]{1,0:T(1,128)S(1)}, f32[1,896]{1,0:T(1,128)S(1)}, f32[1000,896]{1,0:T(8,128)S(1)}) custom-call(bf16[768,896]{1,0:T(8,128)(2,1)S(1)} %get-tuple-element.31.refs_0_, bf16[128,1768]{1,0:T(8,128)(2,1)S(1)} %collective-permute-done.8.refs_1_, bf16[64,1768]{1,0:T(8,128)(2,1)S(1)} %collective-permute-done.7.refs_2_, ...), custom_call_target="tpu_custom_call" | custom-call | tf_op jit(solution)/shard_map/pallas_call | solution.py:111
  23.9 0.4 %collective-permute-done.4.refs_1_ = bf16[64,1768]{1,0:T(8,128)(2,1)S(1)} collective-permute-done((bf16[64,1768]{1,0:T(8,128)(2,1)S(1)}, bf16[64,1768]{1,0:T(8,128)(2,1)S(1)}, u32[]{:S(2)}, u32[]{:S(2)}) %collective-permute-start.4) | collective-permute-done | bytes 226336 | tf_op jit(solution)/shard_map/ppermute | solution.py:127
  24.3 0.1 collective-permute-start.11
  24.4 1.5 %shard_map.41 = (f32[1,896]{1,0:T(1,128)S(1)}, f32[1,896]{1,0:T(1,128)S(1)}, f32[1000,896]{1,0:T(8,128)S(1)}) custom-call(bf16[768,896]{1,0:T(8,128)(2,1)S(1)} %get-tuple-element.31.refs_0_, bf16[128,1768]{1,0:T(8,128)(2,1)S(1)} %collective-permute-done.12.refs_1_, bf16[64,1768]{1,0:T(8,128)(2,1)S(1)} %collective-permute-done.9.refs_2_, ...), custom_call_target="tpu_custom_call" | custom-call | tf_op jit(solution)/shard_map/pallas_call | solution.py:111
  26.0 2.1 %shard_map.42 = bf16[1000,896]{1,0:T(8,128)(2,1)} custom-call(bf16[768,896]{1,0:T(8,128)(2,1)S(1)} %get-tuple-element.31.refs_0_, bf16[64,1768]{1,0:T(8,128)(2,1)S(1)} %collective-permute-done.4.refs_1_, bf16[64,1768]{1,0:T(8,128)(2,1)S(1)} %collective-permute-done.11.refs_2_, f32[1,896]{1,0:T(1,128)S(1)} %get-tuple-element.54.refs_3_, ...), custom_call_target="tpu_custom_call" | custom-call | tf_op jit(solution)/shard_map/pallas_call | solution.py:111
  (13 shorter events, 0.2 us)
Async XLA Ops:
  0.0 6.7 %collective-permute-start = (bf16[64,768]{1,0:T(8,128)(2,1)}, bf16[64,768]{1,0:T(8,128)(2,1)S(1)}, u32[]{:S(2)}, u32[]{:S(2)}) collective-permute-start(bf16[64,768]{1,0:T(8,128)(2,1)} %k_hbm.1), channel_id=1, source_target_pairs={{0,3},{1,4},{4,1},{5,8},{8,5},{9,12},{12,9},{13,14},{14,13},{15,10... | collective-permute-start | bytes 294920 | tf_op jit(solution)/shard_map/ppermute | solution.py:127
  2.4 4.6 %collective-permute-start.1 = (bf16[64,1000]{1,0:T(8,128)(2,1)}, bf16[64,1000]{1,0:T(8,128)(2,1)S(1)}, u32[]{:S(2)}, u32[]{:S(2)}) collective-permute-start(bf16[64,1000]{1,0:T(8,128)(2,1)} %l_hbm.1), channel_id=1, source_target_pairs={{0,3},{1,4},{4,1},{5,8},{8,5},{9,12},{12,9},{13,14},{14,13},{15,10... | collective-permute-start | bytes 384008 | tf_op jit(solution)/shard_map/ppermute | solution.py:127
  4.2 4.8 %collective-permute-start.6 = (bf16[64,1768]{1,0:T(8,128)(2,1)S(1)}, bf16[64,1768]{1,0:T(8,128)(2,1)S(1)}, u32[]{:S(2)}, u32[]{:S(2)}) collective-permute-start(bf16[64,1768]{1,0:T(8,128)(2,1)S(1)} %get-tuple-element.32.refs_1_), channel_id=1, source_target_pairs={{0,1},{1,0},{4,5},{5,4},{8,9},{9,8},{12,13},{13,12},{14,15},{15,14... | collective-permute-start | bytes 678920 | tf_op jit(solution)/shard_map/ppermute | solution.py:127
  5.0 5.4 %collective-permute-start.5 = (bf16[64,1768]{1,0:T(8,128)(2,1)S(1)}, bf16[64,1768]{1,0:T(8,128)(2,1)S(1)}, u32[]{:S(2)}, u32[]{:S(2)}) collective-permute-start(bf16[64,1768]{1,0:T(8,128)(2,1)S(1)} %get-tuple-element.32.refs_1_), channel_id=1, source_target_pairs={{0,5},{1,2},{4,9},{5,0},{8,13},{9,4},{12,15},{13,8},{14,11},{15,12... | collective-permute-start | bytes 678920 | tf_op jit(solution)/shard_map/ppermute | solution.py:127
  7.0 5.8 %collective-permute-start.2 = (bf16[64,1768]{1,0:T(8,128)(2,1)S(1)}, bf16[64,1768]{1,0:T(8,128)(2,1)S(1)}, u32[]{:S(2)}, u32[]{:S(2)}) collective-permute-start(bf16[64,1768]{1,0:T(8,128)(2,1)S(1)} %constant_dynamic-update-slice_fusion.refs_3_), channel_id=1, source_target_pairs={{0,5},{1,2},{4,9},{5,0},{8,13},{9,4},{12,15},{13,8},{14,11},{15,12... | collective-permute-start | bytes 678920 | tf_op jit(solution)/shard_map/ppermute | solution.py:127
  10.4 5.7 %collective-permute-start.7 = (bf16[64,1768]{1,0:T(8,128)(2,1)S(1)}, bf16[64,1768]{1,0:T(8,128)(2,1)S(1)}, u32[]{:S(2)}, u32[]{:S(2)}) collective-permute-start(bf16[64,1768]{1,0:T(8,128)(2,1)S(1)} %collective-permute-done.5.refs_2_), channel_id=1, source_target_pairs={{0,3},{1,4},{4,1},{5,8},{8,5},{9,12},{12,9},{13,14},{14,13},{15,10... | collective-permute-start | bytes 678920 | tf_op jit(solution)/shard_map/ppermute | solution.py:127
  12.4 7.9 %collective-permute-start.10 = (bf16[128,1768]{1,0:T(8,128)(2,1)S(1)}, bf16[128,1768]{1,0:T(8,128)(2,1)S(1)}, u32[]{:S(2)}, u32[]{:S(2)}) collective-permute-start(bf16[128,1768]{1,0:T(8,128)(2,1)S(1)} %pad_maximum_fusion.1), channel_id=1, source_target_pairs={{0,1},{1,0},{4,5},{5,4},{8,9},{9,8},{12,13},{13,12},{14,15},{15,14... | collective-permute-start | bytes 1357832 | tf_op jit(solution)/shard_map/ppermute | solution.py:127
  12.9 5.7 %collective-permute-start.3 = (bf16[64,1768]{1,0:T(8,128)(2,1)S(1)}, bf16[64,1768]{1,0:T(8,128)(2,1)S(1)}, u32[]{:S(2)}, u32[]{:S(2)}) collective-permute-start(bf16[64,1768]{1,0:T(8,128)(2,1)S(1)} %collective-permute-done.2.refs_3_), channel_id=1, source_target_pairs={{0,3},{1,4},{4,1},{5,8},{8,5},{9,12},{12,9},{13,14},{14,13},{15,10... | collective-permute-start | bytes 678920 | tf_op jit(solution)/shard_map/ppermute | solution.py:127
  16.1 5.8 %collective-permute-start.9 = (bf16[64,1768]{1,0:T(8,128)(2,1)S(1)}, bf16[64,1768]{1,0:T(8,128)(2,1)S(1)}, u32[]{:S(2)}, u32[]{:S(2)}) collective-permute-start(bf16[64,1768]{1,0:T(8,128)(2,1)S(1)} %collective-permute-done.7.refs_2_), channel_id=1, source_target_pairs={{0,5},{1,2},{4,9},{5,0},{8,13},{9,4},{12,15},{13,8},{14,11},{15,12... | collective-permute-start | bytes 678920 | tf_op jit(solution)/shard_map/ppermute | solution.py:127
  18.2 4.2 %collective-permute-start.8 = (bf16[128,1768]{1,0:T(8,128)(2,1)S(1)}, bf16[128,1768]{1,0:T(8,128)(2,1)S(1)}, u32[]{:S(2)}, u32[]{:S(2)}) collective-permute-start(bf16[128,1768]{1,0:T(8,128)(2,1)S(1)} %pad_maximum_fusion), channel_id=1, source_target_pairs={{0,1},{1,0},{4,5},{5,4},{8,9},{9,8},{12,13},{13,12},{14,15},{15,14... | collective-permute-start | bytes 1357832 | tf_op jit(solution)/shard_map/ppermute | solution.py:127
  18.5 5.8 %collective-permute-start.4 = (bf16[64,1768]{1,0:T(8,128)(2,1)S(1)}, bf16[64,1768]{1,0:T(8,128)(2,1)S(1)}, u32[]{:S(2)}, u32[]{:S(2)}) collective-permute-start(bf16[64,1768]{1,0:T(8,128)(2,1)S(1)} %collective-permute-done.3.refs_3_), channel_id=1, source_target_pairs={{0,5},{1,2},{4,9},{5,0},{8,13},{9,4},{12,15},{13,8},{14,11},{15,12... | collective-permute-start | bytes 678920 | tf_op jit(solution)/shard_map/ppermute | solution.py:127
  21.9 2.5 %collective-permute-start.12 = (bf16[128,1768]{1,0:T(8,128)(2,1)S(1)}, bf16[128,1768]{1,0:T(8,128)(2,1)S(1)}, u32[]{:S(2)}, u32[]{:S(2)}) collective-permute-start(bf16[128,1768]{1,0:T(8,128)(2,1)S(1)} %pad_maximum_fusion.2), channel_id=1, source_target_pairs={{0,1},{1,0},{4,5},{5,4},{8,9},{9,8},{12,13},{13,12},{14,15},{15,14... | collective-permute-start | bytes 1357832 | tf_op jit(solution)/shard_map/ppermute | solution.py:127
  24.3 1.6 %collective-permute-start.11 = (bf16[64,1768]{1,0:T(8,128)(2,1)S(1)}, bf16[64,1768]{1,0:T(8,128)(2,1)S(1)}, u32[]{:S(2)}, u32[]{:S(2)}) collective-permute-start(bf16[64,1768]{1,0:T(8,128)(2,1)S(1)} %collective-permute-done.4.refs_1_), channel_id=1, source_target_pairs={{0,1},{1,0},{4,5},{5,4},{8,9},{9,8},{12,13},{13,12},{14,15},{15,14... | collective-permute-start | bytes 678920 | tf_op jit(solution)/shard_map/ppermute | solution.py:127
